TPU v7x, 256 devices: a whole 4x4x8 slice. The times are simulated.
256 devices in a mesh: gx: 16 (over z_hi, y), gy: 16 (over z_lo, x, core).
Axes of the slice: x: 4, y: 4, z: 8 (z_hi: 4, z_lo: 2; z = z_hi * 2 + z_lo), core: 2. Of those that a mesh axis runs over, the one named last changes fastest.
Arguments:
- field_e: bfloat16 [3, 192, 384, 128], P(None, 'gx', 'gy'), may hold values from -6 to 6
- field_h: bfloat16 [3, 192, 384, 128], P(None, 'gx', 'gy'), may hold values from -6 to 6
- current: bfloat16 [3, 192, 384, 128], P(None, 'gx', 'gy'), may hold values from -6 to 6
- adjoint_e: bfloat16 [3, 192, 384, 128], P(None, 'gx', 'gy'), may hold values from -6 to 6
- adjoint_h: bfloat16 [3, 192, 384, 128], P(None, 'gx', 'gy'), may hold values from -6 to 6
- adjoint_j: bfloat16 [3, 192, 384, 128], P(None, 'gx', 'gy'), may hold values from -6 to 6
- permittivity: bfloat16 [192, 384, 128], P('gx', 'gy'), may hold values from 1.1953125 to 3
- material: int32 [48, 96, 32], P('gx', 'gy'), may hold values 0 or 1
- design_block: int32 [48, 96, 32], P('gx', 'gy'), may hold values from 0 to 511
Outputs:
- adjoint_e_start: bfloat16 [3, 192, 384, 128], P(None, 'gx', 'gy')
- adjoint_h_start: bfloat16 [3, 192, 384, 128], P(None, 'gx', 'gy')
- adjoint_j_start: bfloat16 [3, 192, 384, 128], P(None, 'gx', 'gy')
- gradient: float32 [512], P(('gx', 'gy'))
All inputs are finite; a program needn't handle non-finite values. No bound on the sum of `material` on one device may be relied on, other than what follows from the above.
Results may differ from a plain program's by a relative error of at most 0.001.
Values sent between devices are 32-bit elements; how exact they have to be, the bound alone decides.
A program may use at most 64 MiB of HBM per device.

v0:
```python
import functools
import math

import jax
import jax.numpy as jnp
import numpy as np
from jax import lax
from jax.experimental import pallas as pl
from jax.experimental.pallas import tpu as pltpu
from jax.sharding import PartitionSpec as P

CB = 3
DT = 0.06
DECAY = 0.96
PLASMA = 16.0
PDT = PLASMA * DT
LIFT = 6.0
MESH = pl.DeviceIdType.MESH
F32 = jnp.float32
BF16 = jnp.bfloat16

EX, EY, EZ = 3, 6, 32
NX, NY, NZ = 4 * EX, 4 * EY, 4 * EZ
ROWS = NX * NY
CHUNK = 4 * NY


def gll_tables():
    points = np.array([-1.0, -math.sqrt(0.2), math.sqrt(0.2), 1.0])
    products = np.array(
        [np.prod([points[i] - points[j] for j in range(4) if j != i]) for i in range(4)]
    )
    matrix = np.zeros((4, 4))
    for i in range(4):
        for j in range(4):
            if i != j:
                matrix[i, j] = products[i] / products[j] / (points[i] - points[j])
    for i in range(4):
        matrix[i, i] = -np.sum(matrix[i])
    return matrix


def line_matrix(elements):
    n = 4 * elements
    full = np.kron(np.eye(elements), 2.0 * gll_tables())
    for e in range(elements):
        lo, hi = 4 * e, 4 * e + 3
        full[hi, hi] -= LIFT
        if hi + 1 < n:
            full[hi, hi + 1] += LIFT
        full[lo, lo] += LIFT
        if lo > 0:
            full[lo, lo - 1] -= LIFT
    return full


def two_parts(matrix):
    high = matrix.astype(np.float32).astype(jnp.bfloat16)
    low = (matrix - high.astype(np.float64)).astype(np.float32).astype(jnp.bfloat16)
    return high, low


def constant_arrays():
    zh, zl = two_parts(line_matrix(EZ).T)
    wz = np.block([[zh, zl], [zh, zl]])
    yh, yl = two_parts(np.kron(np.eye(4), line_matrix(EY)))
    wy = np.block([[yh, yh], [yl, yl]])
    w4 = np.array([1.0, 5.0, 5.0, 1.0])
    wsum = np.kron(np.eye(EZ), w4.reshape(4, 1))
    wt = np.tile(wsum, (1, EY)).astype(jnp.bfloat16)
    wm = np.kron(np.kron(np.eye(EY), w4.reshape(4, 1)), np.ones((1, EZ))).astype(np.float32)
    return wz, wy, wt, wm


def split(value):
    high = value.astype(BF16)
    low = (value - high.astype(F32)).astype(BF16)
    return high, low


def curl_chunk(src, ex, wz_ref, wy_ref, exact=False):
    r0 = CHUNK * ex
    comps = [src[c, r0 : r0 + CHUNK, :] for c in range(3)]
    if exact:
        high = [v.astype(BF16) for v in comps]
        zin = jnp.concatenate([high[0], high[1]], axis=0)
        zout = jnp.dot(zin, wz_ref[0:NZ, :], preferred_element_type=F32)
        yin = jnp.concatenate([high[0], high[2]], axis=1)
        yout = jnp.dot(wy_ref[:, 0:CHUNK], yin, preferred_element_type=F32)
    else:
        high, low = zip(*[split(v) for v in comps])
        zin = jnp.concatenate(
            [
                jnp.concatenate([high[0], low[0]], axis=1),
                jnp.concatenate([high[1], low[1]], axis=1),
            ],
            axis=0,
        )
        zout = jnp.dot(zin, wz_ref[...], preferred_element_type=F32)
        yin = jnp.concatenate(
            [
                jnp.concatenate([high[0], high[2]], axis=1),
                jnp.concatenate([low[0], low[2]], axis=1),
            ],
            axis=0,
        )
        yout = jnp.dot(wy_ref[...], yin, preferred_element_type=F32)
    zsum = zout[:, 0:NZ] + zout[:, NZ : 2 * NZ]
    dz_x, dz_y = zsum[0:CHUNK], zsum[CHUNK : 2 * CHUNK]
    ysum = yout[0:CHUNK] + yout[CHUNK : 2 * CHUNK]
    dy_x, dy_z = ysum[:, 0:NZ], ysum[:, NZ : 2 * NZ]

    m = 2.0 * gll_tables()

    def along_x(c):
        p = [comps[c][NY * a : NY * (a + 1)] for a in range(4)]
        out0 = m[0, 1] * p[1] + m[0, 2] * p[2] + m[0, 3] * p[3]
        if ex > 0:
            out0 = out0 - LIFT * src[c, r0 - NY : r0, :]
        out1 = m[1, 0] * p[0] + m[1, 2] * p[2] + m[1, 3] * p[3]
        out2 = m[2, 0] * p[0] + m[2, 1] * p[1] + m[2, 3] * p[3]
        out3 = m[3, 0] * p[0] + m[3, 1] * p[1] + m[3, 2] * p[2]
        if ex < EX - 1:
            out3 = out3 + LIFT * src[c, r0 + CHUNK : r0 + CHUNK + NY, :]
        return jnp.concatenate([out0, out1, out2, out3], axis=0)

    dx_y, dx_z = along_x(1), along_x(2)
    return dy_z - dz_y, dz_x - dx_z, dx_y - dy_x


def kernel(
    n_gx,
    n_gy,
    e_in, h_in, j_in, le_in, lh_in, lj_in, eps_in, mat_in, blk_in, wz_in, wy_in, wt_in, wm_in,
    oe_out, oh_out, oj_out, grad_ref,
    eb, hb, jb, leb, lhb, ljb, epsb, mat, blk, wz, wy, wt, wm,
    e0, h1, e1, h2, d1, tot1, sc1, mid1, tot0, sc0, mid0, le0, lj1,
    step, drude, part, onehot, oeb, ohb, ojb,
    ys, xr, yr, gsend, grecv, msend, mrecv,
    in_sem, out_sem, send_sem, recv_sem, g_send_sem, g_recv_sem, m_send_sem, m_recv_sem,
):
    gx, gy = lax.axis_index("gx"), lax.axis_index("gy")

    def load(index, src, dst):
        copy = pltpu.make_async_copy(src, dst, in_sem.at[index])
        copy.start()
        return copy

    in_e = load(0, e_in, eb)
    in_le = load(1, le_in, leb)
    in_lj = load(2, lj_in, ljb)
    in_eps = load(3, eps_in, epsb)
    in_mat = load(4, mat_in, mat)
    in_wz = load(5, wz_in, wz)
    in_wy = load(6, wy_in, wy)
    in_h = load(7, h_in, hb)
    in_lh = load(8, lh_in, lhb)
    in_j = load(9, j_in, jb)
    in_blk = load(10, blk_in, blk)
    in_wt = load(11, wt_in, wt)
    in_wm = load(12, wm_in, wm)

    barrier = pltpu.get_barrier_semaphore()
    for k in range(1, n_gx):
        pl.semaphore_signal(
            barrier, inc=1, device_id=(lax.rem(gx + k, n_gx), gy), device_id_type=MESH
        )
    for k in range(1, n_gy):
        pl.semaphore_signal(
            barrier, inc=1, device_id=(gx, lax.rem(gy + k, n_gy)), device_id_type=MESH
        )

    right = (lax.rem(gx + 1, n_gx), gy)
    left = (lax.rem(gx + n_gx - 1, n_gx), gy)
    up = (gx, lax.rem(gy + 1, n_gy))
    down = (gx, lax.rem(gy + n_gy - 1, n_gy))
    first_y = pl.ds(0, NX, stride=NY)
    last_y = pl.ds(NY - 1, NX, stride=NY)
    first_x = slice(0, NY)
    last_x = slice(ROWS - NY, ROWS)

    def stage_y(k, field):
        ys[k, 0, 0] = field[0, first_y, :]
        ys[k, 0, 1] = field[2, first_y, :]
        ys[k, 1, 0] = field[0, last_y, :]
        ys[k, 1, 1] = field[2, last_y, :]

    def send(k, field):
        plan = (
            (field.at[pl.ds(1, 2), pl.ds(ROWS - NY, NY)], xr.at[k, 0], right),
            (field.at[pl.ds(1, 2), pl.ds(0, NY)], xr.at[k, 1], left),
            (ys.at[k, 1], yr.at[k, 0], up),
            (ys.at[k, 0], yr.at[k, 1], down),
        )
        copies = []
        for i, (src, dst, target) in enumerate(plan):
            copy = pltpu.make_async_remote_copy(
                src_ref=src, dst_ref=dst, send_sem=send_sem.at[k, i], recv_sem=recv_sem.at[k, i],
                device_id=target, device_id_type=MESH,
            )
            copy.start()
            copies.append(copy)
        return copies

    def arrived(copies):
        for copy in copies:
            copy.wait_recv()

    def fix(k, field, factor):
        f = factor(first_x) * LIFT
        field[1, first_x, :] += f * xr[k, 0, 1]
        field[2, first_x, :] -= f * xr[k, 0, 0]
        f = factor(last_x) * LIFT
        field[1, last_x, :] -= f * xr[k, 1, 1]
        field[2, last_x, :] += f * xr[k, 1, 0]
        f = factor(first_y) * LIFT
        field[0, first_y, :] -= f * yr[k, 0, 1]
        field[2, first_y, :] += f * yr[k, 0, 0]
        f = factor(last_y) * LIFT
        field[0, last_y, :] += f * yr[k, 1, 1]
        field[2, last_y, :] -= f * yr[k, 1, 0]

    by_dt = lambda rows: -DT
    by_one = lambda rows: 1.0
    by_step = lambda rows: step[rows, :]
    by_step_dt = lambda rows: -DT * step[rows, :]

    def chunks():
        return [(ex, slice(CHUNK * ex, CHUNK * (ex + 1))) for ex in range(EX)]

    in_e.wait()
    for c in range(3):
        e0[c] = eb[c].astype(F32)
    stage_y(0, e0)
    pl.semaphore_wait(barrier, n_gx + n_gy - 2)
    f1 = send(0, e0)

    in_mat.wait()
    in_eps.wait()
    zpick = (
        lax.broadcasted_iota(jnp.int32, (EZ, NZ), 0) == lax.broadcasted_iota(jnp.int32, (EZ, NZ), 1) >> 2
    ).astype(F32).astype(BF16)
    ypick = (
        lax.broadcasted_iota(jnp.int32, (NY, EY), 0) >> 2 == lax.broadcasted_iota(jnp.int32, (NY, EY), 1)
    ).astype(F32).astype(BF16)
    for ex, rows in chunks():
        picked = jnp.dot(mat[ex].astype(F32).astype(BF16), zpick, preferred_element_type=F32)
        plane = jnp.dot(ypick, picked.astype(BF16), preferred_element_type=F32)
        for a in range(4):
            drude[CHUNK * ex + NY * a : CHUNK * ex + NY * (a + 1), :] = plane
    step[...] = DT / epsb[...].astype(F32)
    in_le.wait()
    in_lj.wait()
    for c in range(3):
        total = leb[c].astype(F32) + PDT * drude[...] * ljb[c].astype(F32)
        tot1[c] = total
        sc1[c] = step[...] * total
    stage_y(1, sc1)
    a1 = send(1, sc1)

    in_wz.wait()
    in_wy.wait()
    in_h.wait()
    for ex, rows in chunks():
        curl = curl_chunk(e0, ex, wz, wy, exact=True)
        for c in range(3):
            h1[c, rows, :] = hb[c, rows, :].astype(F32) - DT * curl[c]
    in_lh.wait()
    for ex, rows in chunks():
        curl = curl_chunk(sc1, ex, wz, wy)
        for c in range(3):
            mid1[c, rows, :] = lhb[c, rows, :].astype(F32) + curl[c]

    arrived(f1)
    fix(0, h1, by_dt)
    stage_y(2, h1)
    f2 = send(2, h1)
    arrived(a1)
    fix(1, mid1, by_one)
    stage_y(3, mid1)
    a2 = send(3, mid1)

    in_j.wait()
    for ex, rows in chunks():
        curl = curl_chunk(h1, ex, wz, wy)
        for c in range(3):
            e1[c, rows, :] = e0[c, rows, :] + step[rows, :] * (
                curl[c] - drude[rows, :] * jb[c, rows, :].astype(F32)
            )
    for ex, rows in chunks():
        curl = curl_chunk(mid1, ex, wz, wy)
        for c in range(3):
            lj = drude[rows, :] * (DECAY * ljb[c, rows, :].astype(F32) - sc1[c, rows, :])
            lj1[c, rows, :] = lj
            total = tot1[c, rows, :] - DT * curl[c] + PDT * lj
            tot0[c, rows, :] = total
            sc0[c, rows, :] = step[rows, :] * total

    arrived(f2)
    fix(2, e1, by_step)
    stage_y(4, e1)
    f3 = send(4, e1)
    arrived(a2)
    fix(3, tot0, by_dt)
    fix(3, sc0, by_step_dt)
    stage_y(5, sc0)
    a3 = send(5, sc0)

    for ex, rows in chunks():
        curl = curl_chunk(e1, ex, wz, wy)
        for c in range(3):
            h2[c, rows, :] = h1[c, rows, :] - DT * curl[c]
    for ex, rows in chunks():
        curl = curl_chunk(sc0, ex, wz, wy)
        for c in range(3):
            mid0[c, rows, :] = mid1[c, rows, :] + curl[c]

    in_blk.wait()
    eye = lax.broadcasted_iota(jnp.int32, (EZ, EZ), 0) == lax.broadcasted_iota(jnp.int32, (EZ, EZ), 1)
    ones = jnp.ones((EZ, 128), BF16)
    n_rows = gsend.shape[0]
    lane = lax.broadcasted_iota(jnp.int32, (EY * EZ, 128), 1)
    for ex in range(EX):
        ids = blk[ex]
        coarse, fine = (ids & -16).astype(F32), (ids & 15).astype(F32)
        wide = jnp.concatenate(
            [jnp.where(eye, coarse[ey : ey + 1, :], 0.0) for ey in range(EY)], axis=0
        ).astype(BF16)
        narrow = jnp.concatenate(
            [jnp.where(eye, fine[ey : ey + 1, :], 0.0) for ey in range(EY)], axis=0
        ).astype(BF16)
        column = jnp.dot(wide, ones, preferred_element_type=F32) + jnp.dot(
            narrow, ones, preferred_element_type=F32
        )
        column = column.astype(jnp.int32)
        for q in range(n_rows):
            onehot[ex, :, 128 * q : 128 * (q + 1)] = (
                (column == lane + 128 * q).astype(F32).astype(BF16)
            )

    arrived(f3)
    fix(4, h2, by_dt)
    stage_y(6, h2)
    f4 = send(6, h2)
    arrived(a3)
    fix(5, mid0, by_one)
    stage_y(7, mid0)
    a4 = send(7, mid0)

    for c in range(3):
        ohb[c] = mid0[c].astype(BF16)
    out_h = pltpu.make_async_copy(ohb, oh_out, out_sem.at[0])
    out_h.start()
    for c in range(3):
        ojb[c] = (drude[...] * (DECAY * lj1[c] - sc0[c])).astype(BF16)
    out_j = pltpu.make_async_copy(ojb, oj_out, out_sem.at[1])
    out_j.start()

    for ex, rows in chunks():
        curl = curl_chunk(h2, ex, wz, wy)
        for c in range(3):
            current = drude[rows, :] * (DECAY * jb[c, rows, :].astype(F32) + PDT * e1[c, rows, :])
            d1[c, rows, :] = step[rows, :] * (curl[c] - current)
    part[...] = (
        tot0[0] * (e1[0] - e0[0]) + tot0[1] * (e1[1] - e0[1]) + tot0[2] * (e1[2] - e0[2])
    )
    for ex, rows in chunks():
        curl = curl_chunk(mid0, ex, wz, wy)
        for c in range(3):
            le0[c, rows, :] = tot0[c, rows, :] - DT * curl[c]

    in_wt.wait()
    in_wm.wait()
    arrived(f4)
    fix(6, d1, by_step)
    sums = jnp.zeros((16, 128 * n_rows), F32)
    row16 = lax.broadcasted_iota(jnp.int32, (16, EY * EZ), 0)
    scale = -1.0 / (216.0 * 8.0 * DT)
    for ex, rows in chunks():
        node = part[rows, :]
        for c in range(3):
            node = node + tot1[c, rows, :] * d1[c, rows, :]
        node = node * step[rows, :]
        layer = (
            node[0:NY] + 5.0 * node[NY : 2 * NY] + 5.0 * node[2 * NY : 3 * NY] + node[3 * NY : 4 * NY]
        )
        high = layer.astype(BF16)
        rest = layer - high.astype(F32)
        mid = rest.astype(BF16)
        low = (rest - mid.astype(F32)).astype(BF16)
        wide = (
            jnp.dot(high, wt[...], preferred_element_type=F32)
            + jnp.dot(mid, wt[...], preferred_element_type=F32)
            + jnp.dot(low, wt[...], preferred_element_type=F32)
        )
        flat = jnp.sum(wide * wm[...], axis=0, keepdims=True)
        flat = jnp.broadcast_to(flat * scale, (16, EY * EZ))
        top = flat.astype(BF16).astype(F32)
        rest = flat - top
        mid = rest.astype(BF16).astype(F32)
        pieces = jnp.where(
            row16 == 0, top, jnp.where(row16 == 1, mid, jnp.where(row16 == 2, rest - mid, 0.0))
        ).astype(BF16)
        sums = sums + jnp.dot(pieces, onehot[ex], preferred_element_type=F32)
    total = jnp.sum(sums, axis=0, keepdims=True)
    for q in range(n_rows):
        gsend[q] = total[:, 128 * q : 128 * (q + 1)]
    width = 2 * n_gy
    per_row = 128 // width
    phase1 = []
    for k in range(1, n_gx):
        p = lax.rem(gx + k, n_gx)
        copy = pltpu.make_async_remote_copy(
            src_ref=gsend.at[lax.div(p, per_row)], dst_ref=grecv.at[k],
            send_sem=g_send_sem.at[k], recv_sem=g_recv_sem.at[k],
            device_id=(p, gy), device_id_type=MESH,
        )
        copy.start()
        phase1.append(copy)

    arrived(a4)
    fix(7, le0, by_dt)
    for c in range(3):
        oeb[c] = le0[c].astype(BF16)
    out_e = pltpu.make_async_copy(oeb, oe_out, out_sem.at[2])
    out_e.start()

    mine = gsend[lax.div(gx, per_row)]
    arrived(phase1)
    for k in range(1, n_gx):
        mine = mine + grecv[k]
    msend[...] = mine
    phase2 = []
    for k in range(1, n_gy):
        copy = pltpu.make_async_remote_copy(
            src_ref=msend, dst_ref=mrecv.at[k],
            send_sem=m_send_sem.at[k], recv_sem=m_recv_sem.at[k],
            device_id=(gx, lax.rem(gy + k, n_gy)), device_id_type=MESH,
        )
        copy.start()
        phase2.append(copy)
    for copies in (f1, a1, f2, a2, f3, a3, f4, a4, phase1):
        for copy in copies:
            copy.wait_send()
    out_h.wait()
    out_j.wait()
    out_e.wait()
    arrived(phase2)
    for k in range(1, n_gy):
        mine = mine + mrecv[k]
    at = lax.rem(gx, per_row) * width + 2 * gy
    lanes = lax.broadcasted_iota(jnp.int32, (1, 128), 1)
    first = jnp.sum(jnp.where(lanes == at, mine, 0.0), axis=1, keepdims=True)
    second = jnp.sum(jnp.where(lanes == at + 1, mine, 0.0), axis=1, keepdims=True)
    grad_ref[...] = jnp.where(lanes == 0, first, second)
    for copy in phase2:
        copy.wait_send()


def per_device(n_gx, n_gy, *args):
    fields = [a.reshape(3, ROWS, NZ) for a in args[0:6]]
    eps = args[6].reshape(ROWS, NZ)
    blocks = EX * n_gx // CB * (EY * n_gy // CB)
    n_rows = -(-blocks // 128)
    consts = [jnp.asarray(a) for a in constant_arrays()]
    hbm = pl.BlockSpec(memory_space=pl.ANY)
    field32 = pltpu.VMEM((3, ROWS, NZ), F32)
    field16 = pltpu.VMEM((3, ROWS, NZ), BF16)
    plane32 = pltpu.VMEM((ROWS, NZ), F32)
    out16 = jax.ShapeDtypeStruct((3, ROWS, NZ), BF16)
    oe, oh, oj, grad = pl.pallas_call(
        functools.partial(kernel, n_gx, n_gy),
        out_shape=(out16, out16, out16, jax.ShapeDtypeStruct((1, 128), F32)),
        in_specs=[hbm] * 13,
        out_specs=(hbm, hbm, hbm, pl.BlockSpec(memory_space=pltpu.VMEM)),
        scratch_shapes=[
            *[field16] * 6,
            pltpu.VMEM((ROWS, NZ), BF16),
            pltpu.VMEM((EX, EY, EZ), jnp.int32),
            pltpu.VMEM((EX, EY, EZ), jnp.int32),
            *[pltpu.VMEM(a.shape, a.dtype) for a in consts],
            *[field32] * 13,
            plane32,
            plane32,
            plane32,
            pltpu.VMEM((EX, EY * EZ, 128 * n_rows), BF16),
            *[field16] * 3,
            pltpu.VMEM((8, 2, 2, NX, NZ), F32),
            pltpu.VMEM((8, 2, 2, NY, NZ), F32),
            pltpu.VMEM((8, 2, 2, NX, NZ), F32),
            pltpu.VMEM((n_rows, 1, 128), F32),
            pltpu.VMEM((n_gx, 1, 128), F32),
            pltpu.VMEM((1, 128), F32),
            pltpu.VMEM((n_gy, 1, 128), F32),
            pltpu.SemaphoreType.DMA((13,)),
            pltpu.SemaphoreType.DMA((3,)),
            pltpu.SemaphoreType.DMA((8, 4)),
            pltpu.SemaphoreType.DMA((8, 4)),
            pltpu.SemaphoreType.DMA((n_gx,)),
            pltpu.SemaphoreType.DMA((n_gx,)),
            pltpu.SemaphoreType.DMA((n_gy,)),
            pltpu.SemaphoreType.DMA((n_gy,)),
        ],
        compiler_params=pltpu.CompilerParams(
            collective_id=0, has_side_effects=True, vmem_limit_bytes=48 * 1024 * 1024
        ),
    )(*fields, eps, args[7], args[8], *consts)
    shape = args[0].shape
    return oe.reshape(shape), oh.reshape(shape), oj.reshape(shape), grad[0, 0:2]


def solution(mesh):
    n_gx, n_gy = mesh.shape["gx"], mesh.shape["gy"]
    field = P(None, "gx", "gy", None)
    node = P("gx", "gy", None)
    return jax.shard_map(
        functools.partial(per_device, n_gx, n_gy),
        mesh=mesh,
        in_specs=(field,) * 6 + (node,) * 3,
        out_specs=(field, field, field, P(("gx", "gy"))),
        check_vma=False,
    )
```

profile of v0, /device:TPU:1, one launch (start us, length us, event | category | flops | bytes accessed | tf_op | source)
XLA Modules:
  0.0 58.2 jit_solution(15280983786898356746)
XLA Ops:
  0.6 0.0 copy-start.11
  0.6 0.7 %copy-done.11 = s32[3,6,32]{2,1,0:T(8,128)S(1)} copy-done((s32[3,6,32]{2,1,0:T(8,128)S(1)}, s32[3,6,32]{2,1,0:T(8,128)}, u32[]{:S(2)}) %copy-start.11) | copy-done | bytes 2328
  1.3 0.0 copy-start
  1.3 0.9 %copy-done = bf16[3,12,24,128]{3,2,1,0:T(8,128)(2,1)S(1)} copy-done((bf16[3,12,24,128]{3,2,1,0:T(8,128)(2,1)S(1)}, bf16[3,12,24,128]{3,2,1,0:T(8,128)(2,1)}, u32[]{:S(2)}) %copy-start) | copy-done | bytes 221208
  2.3 0.0 copy-start.1
  2.3 0.9 %copy-done.1 = bf16[3,12,24,128]{3,2,1,0:T(8,128)(2,1)S(1)} copy-done((bf16[3,12,24,128]{3,2,1,0:T(8,128)(2,1)S(1)}, bf16[3,12,24,128]{3,2,1,0:T(8,128)(2,1)}, u32[]{:S(2)}) %copy-start.1) | copy-done | bytes 221208
  3.2 0.0 copy-start.2
  3.2 0.9 %copy-done.2 = bf16[3,12,24,128]{3,2,1,0:T(8,128)(2,1)S(1)} copy-done((bf16[3,12,24,128]{3,2,1,0:T(8,128)(2,1)S(1)}, bf16[3,12,24,128]{3,2,1,0:T(8,128)(2,1)}, u32[]{:S(2)}) %copy-start.2) | copy-done | bytes 221208
  4.2 0.0 copy-start.3
  4.2 0.9 %copy-done.3 = bf16[3,12,24,128]{3,2,1,0:T(8,128)(2,1)S(1)} copy-done((bf16[3,12,24,128]{3,2,1,0:T(8,128)(2,1)S(1)}, bf16[3,12,24,128]{3,2,1,0:T(8,128)(2,1)}, u32[]{:S(2)}) %copy-start.3) | copy-done | bytes 221208
  5.1 0.0 copy-start.4
  5.1 0.9 %copy-done.4 = bf16[3,12,24,128]{3,2,1,0:T(8,128)(2,1)S(1)} copy-done((bf16[3,12,24,128]{3,2,1,0:T(8,128)(2,1)S(1)}, bf16[3,12,24,128]{3,2,1,0:T(8,128)(2,1)}, u32[]{:S(2)}) %copy-start.4) | copy-done | bytes 221208
  6.0 0.0 copy-start.5
  6.0 0.9 %copy-done.5 = bf16[3,12,24,128]{3,2,1,0:T(8,128)(2,1)S(1)} copy-done((bf16[3,12,24,128]{3,2,1,0:T(8,128)(2,1)S(1)}, bf16[3,12,24,128]{3,2,1,0:T(8,128)(2,1)}, u32[]{:S(2)}) %copy-start.5) | copy-done | bytes 221208
  7.0 0.0 copy-start.6
  7.0 0.9 %copy-done.6 = bf16[256,256]{1,0:T(8,128)(2,1)S(1)} copy-done((bf16[256,256]{1,0:T(8,128)(2,1)S(1)}, bf16[256,256]{1,0:T(8,128)(2,1)}, u32[]{:S(2)}) %copy-start.6) | copy-done | bytes 131096
  7.9 0.0 copy-start.7
  7.9 0.9 %copy-done.7 = bf16[192,192]{1,0:T(8,128)(2,1)S(1)} copy-done((bf16[192,192]{1,0:T(8,128)(2,1)S(1)}, bf16[192,192]{1,0:T(8,128)(2,1)}, u32[]{:S(2)}) %copy-start.7) | copy-done | bytes 73752
  8.8 0.0 copy-start.8
  8.8 0.9 %copy-done.8 = bf16[12,24,128]{2,1,0:T(8,128)(2,1)S(1)} copy-done((bf16[12,24,128]{2,1,0:T(8,128)(2,1)S(1)}, bf16[12,24,128]{2,1,0:T(8,128)(2,1)}, u32[]{:S(2)}) %copy-start.8) | copy-done | bytes 73752
  9.6 0.0 copy-start.9
  9.6 0.8 %copy-done.9 = bf16[128,192]{1,0:T(8,128)(2,1)S(1)} copy-done((bf16[128,192]{1,0:T(8,128)(2,1)S(1)}, bf16[128,192]{1,0:T(8,128)(2,1)}, u32[]{:S(2)}) %copy-start.9) | copy-done | bytes 49176
  10.5 0.0 copy-start.10
  10.5 0.7 %copy-done.10 = f32[24,192]{1,0:T(8,128)S(1)} copy-done((f32[24,192]{1,0:T(8,128)S(1)}, f32[24,192]{1,0:T(8,128)}, u32[]{:S(2)}) %copy-start.10) | copy-done | bytes 18456
  11.2 0.0 copy-start.12
  11.2 0.7 %copy-done.12 = s32[3,6,32]{2,1,0:T(8,128)S(1)} copy-done((s32[3,6,32]{2,1,0:T(8,128)S(1)}, s32[3,6,32]{2,1,0:T(8,128)}, u32[]{:S(2)}) %copy-start.12) | copy-done | bytes 2328
  11.9 43.7 %shard_map.156 = (bf16[3,288,128]{2,1,0:T(8,128)(2,1)S(1)}, bf16[3,288,128]{2,1,0:T(8,128)(2,1)S(1)}, bf16[3,288,128]{2,1,0:T(8,128)(2,1)S(1)}, f32[1,128]{1,0:T(1,128)S(1)}) custom-call(bf16[3,288,128]{2,1,0:T(8,128)(2,1)S(1)} %bitcast.15, bf16[3,288,128]{2,1,0:T(8,128)(2,1)S(1)} %bitcast.16, bf16[3,288,128]{2,1,0:T(8,128)(2,1)S(1)} %bitcast.17, ...), custom_call_target="tpu_custom_call" | custom-call | tf_op jit(solution)/shard_map/pallas_call | solution.py:471
  55.7 0.5 slice_bitcast_fusion
  56.2 0.7 %copy.20 = bf16[3,12,24,128]{3,2,1,0:T(8,128)(2,1)} copy(bf16[3,12,24,128]{3,2,1,0:T(8,128)(2,1)S(1)} %bitcast.14) | data formatting | bytes 442368
  56.9 0.7 %copy.21 = bf16[3,12,24,128]{3,2,1,0:T(8,128)(2,1)} copy(bf16[3,12,24,128]{3,2,1,0:T(8,128)(2,1)S(1)} %bitcast.13) | data formatting | bytes 442368
  57.5 0.7 %copy.22 = bf16[3,12,24,128]{3,2,1,0:T(8,128)(2,1)} copy(bf16[3,12,24,128]{3,2,1,0:T(8,128)(2,1)S(1)} %bitcast.12) | data formatting | bytes 442368
Async XLA Ops:
  0.6 0.7 %copy-start.11 = (s32[3,6,32]{2,1,0:T(8,128)S(1)}, s32[3,6,32]{2,1,0:T(8,128)}, u32[]{:S(2)}) copy-start(s32[3,6,32]{2,1,0:T(8,128)} %mat_in.1) | copy-start | bytes 6916
  1.3 0.9 %copy-start = (bf16[3,12,24,128]{3,2,1,0:T(8,128)(2,1)S(1)}, bf16[3,12,24,128]{3,2,1,0:T(8,128)(2,1)}, u32[]{:S(2)}) copy-start(bf16[3,12,24,128]{3,2,1,0:T(8,128)(2,1)} %param.13) | copy-start | bytes 663556
  2.3 0.9 %copy-start.1 = (bf16[3,12,24,128]{3,2,1,0:T(8,128)(2,1)S(1)}, bf16[3,12,24,128]{3,2,1,0:T(8,128)(2,1)}, u32[]{:S(2)}) copy-start(bf16[3,12,24,128]{3,2,1,0:T(8,128)(2,1)} %param.14) | copy-start | bytes 663556
  3.2 0.9 %copy-start.2 = (bf16[3,12,24,128]{3,2,1,0:T(8,128)(2,1)S(1)}, bf16[3,12,24,128]{3,2,1,0:T(8,128)(2,1)}, u32[]{:S(2)}) copy-start(bf16[3,12,24,128]{3,2,1,0:T(8,128)(2,1)} %param.15) | copy-start | bytes 663556
  4.2 0.9 %copy-start.3 = (bf16[3,12,24,128]{3,2,1,0:T(8,128)(2,1)S(1)}, bf16[3,12,24,128]{3,2,1,0:T(8,128)(2,1)}, u32[]{:S(2)}) copy-start(bf16[3,12,24,128]{3,2,1,0:T(8,128)(2,1)} %param.16) | copy-start | bytes 663556
  5.1 0.9 %copy-start.4 = (bf16[3,12,24,128]{3,2,1,0:T(8,128)(2,1)S(1)}, bf16[3,12,24,128]{3,2,1,0:T(8,128)(2,1)}, u32[]{:S(2)}) copy-start(bf16[3,12,24,128]{3,2,1,0:T(8,128)(2,1)} %param.17) | copy-start | bytes 663556
  6.0 0.9 %copy-start.5 = (bf16[3,12,24,128]{3,2,1,0:T(8,128)(2,1)S(1)}, bf16[3,12,24,128]{3,2,1,0:T(8,128)(2,1)}, u32[]{:S(2)}) copy-start(bf16[3,12,24,128]{3,2,1,0:T(8,128)(2,1)} %param.18) | copy-start | bytes 663556
  7.0 0.9 %copy-start.6 = (bf16[256,256]{1,0:T(8,128)(2,1)S(1)}, bf16[256,256]{1,0:T(8,128)(2,1)}, u32[]{:S(2)}) copy-start(bf16[256,256]{1,0:T(8,128)(2,1)} %constant.8.clone.wz_in) | copy-start | bytes 393220
  7.9 0.9 %copy-start.7 = (bf16[192,192]{1,0:T(8,128)(2,1)S(1)}, bf16[192,192]{1,0:T(8,128)(2,1)}, u32[]{:S(2)}) copy-start(bf16[192,192]{1,0:T(8,128)(2,1)} %constant.9.clone.wy_in) | copy-start | bytes 221188
  8.8 0.9 %copy-start.8 = (bf16[12,24,128]{2,1,0:T(8,128)(2,1)S(1)}, bf16[12,24,128]{2,1,0:T(8,128)(2,1)}, u32[]{:S(2)}) copy-start(bf16[12,24,128]{2,1,0:T(8,128)(2,1)} %param.19) | copy-start | bytes 221188
  9.6 0.8 %copy-start.9 = (bf16[128,192]{1,0:T(8,128)(2,1)S(1)}, bf16[128,192]{1,0:T(8,128)(2,1)}, u32[]{:S(2)}) copy-start(bf16[128,192]{1,0:T(8,128)(2,1)} %constant.10.clone.wt_in) | copy-start | bytes 147460
  10.5 0.7 %copy-start.10 = (f32[24,192]{1,0:T(8,128)S(1)}, f32[24,192]{1,0:T(8,128)}, u32[]{:S(2)}) copy-start(f32[24,192]{1,0:T(8,128)} %constant.11.clone.wm_in) | copy-start | bytes 55300
  11.2 0.7 %copy-start.12 = (s32[3,6,32]{2,1,0:T(8,128)S(1)}, s32[3,6,32]{2,1,0:T(8,128)}, u32[]{:S(2)}) copy-start(s32[3,6,32]{2,1,0:T(8,128)} %blk_in.1) | copy-start | bytes 6916
where the time goes:
time: 58.8 us; the launch traced here: 58.2 us
  Pallas kernels  43.7 us (74%)
  local copies, waits for them, and re-layouts  13.8 us (23%)
  between operations  0.66 us (1%)
    pallas_call x1, Pallas kernels, per_device(): pl.pallas_call(functools.partial(kernel, n_gx, n_gy), out_shape=(out16, o...  43.7 us
    unnamed x29, local copies, waits for them, and re-layouts  13.3 us

commit v1 on v0

v1 whole, which is shorter than its diff:
```python
import functools
import math

import jax
import jax.numpy as jnp
import numpy as np
from jax import lax
from jax.experimental import pallas as pl
from jax.experimental.pallas import tpu as pltpu
from jax.sharding import PartitionSpec as P

CB = 3
DT = 0.06
DECAY = 0.96
PLASMA = 16.0
PDT = PLASMA * DT
LIFT = 6.0
MESH = pl.DeviceIdType.MESH
F32 = jnp.float32
BF16 = jnp.bfloat16

EX, EY, EZ = 3, 6, 32
NX, NY, NZ = 4 * EX, 4 * EY, 4 * EZ
ROWS = NX * NY
CHUNK = 4 * NY


def gll_tables():
    points = np.array([-1.0, -math.sqrt(0.2), math.sqrt(0.2), 1.0])
    products = np.array(
        [np.prod([points[i] - points[j] for j in range(4) if j != i]) for i in range(4)]
    )
    matrix = np.zeros((4, 4))
    for i in range(4):
        for j in range(4):
            if i != j:
                matrix[i, j] = products[i] / products[j] / (points[i] - points[j])
    for i in range(4):
        matrix[i, i] = -np.sum(matrix[i])
    return matrix


def line_matrix(elements):
    n = 4 * elements
    full = np.kron(np.eye(elements), 2.0 * gll_tables())
    for e in range(elements):
        lo, hi = 4 * e, 4 * e + 3
        full[hi, hi] -= LIFT
        if hi + 1 < n:
            full[hi, hi + 1] += LIFT
        full[lo, lo] += LIFT
        if lo > 0:
            full[lo, lo - 1] -= LIFT
    return full


def two_parts(matrix):
    high = matrix.astype(np.float32).astype(jnp.bfloat16)
    low = (matrix - high.astype(np.float64)).astype(np.float32).astype(jnp.bfloat16)
    return high, low


def constant_arrays():
    zh, zl = two_parts(line_matrix(EZ).T)
    wz = np.block([[zh, zl], [zh, zl]])
    yh, yl = two_parts(np.kron(np.eye(4), line_matrix(EY)))
    wy = np.block([[yh, yh], [yl, yl]])
    w4 = np.array([1.0, 5.0, 5.0, 1.0])
    wsum = np.kron(np.eye(EZ), w4.reshape(4, 1))
    wt = np.tile(wsum, (1, EY)).astype(jnp.bfloat16)
    wm = np.kron(np.kron(np.eye(EY), w4.reshape(4, 1)), np.ones((1, EZ))).astype(np.float32)
    return wz, wy, wt, wm


def split(value):
    high = value.astype(BF16)
    low = (value - high.astype(F32)).astype(BF16)
    return high, low


def curl_chunk(src, ex, wz_ref, wy_ref, exact=False):
    r0 = CHUNK * ex
    comps = [src[c, r0 : r0 + CHUNK, :] for c in range(3)]
    if exact:
        high = [v.astype(BF16) for v in comps]
        zin = jnp.concatenate([high[0], high[1]], axis=0)
        zout = jnp.dot(zin, wz_ref[0:NZ, :], preferred_element_type=F32)
        yin = jnp.concatenate([high[0], high[2]], axis=1)
        yout = jnp.dot(wy_ref[:, 0:CHUNK], yin, preferred_element_type=F32)
    else:
        high, low = zip(*[split(v) for v in comps])
        zin = jnp.concatenate(
            [
                jnp.concatenate([high[0], low[0]], axis=1),
                jnp.concatenate([high[1], low[1]], axis=1),
            ],
            axis=0,
        )
        zout = jnp.dot(zin, wz_ref[...], preferred_element_type=F32)
        yin = jnp.concatenate(
            [
                jnp.concatenate([high[0], high[2]], axis=1),
                jnp.concatenate([low[0], low[2]], axis=1),
            ],
            axis=0,
        )
        yout = jnp.dot(wy_ref[...], yin, preferred_element_type=F32)
    zsum = zout[:, 0:NZ] + zout[:, NZ : 2 * NZ]
    dz_x, dz_y = zsum[0:CHUNK], zsum[CHUNK : 2 * CHUNK]
    ysum = yout[0:CHUNK] + yout[CHUNK : 2 * CHUNK]
    dy_x, dy_z = ysum[:, 0:NZ], ysum[:, NZ : 2 * NZ]

    m = 2.0 * gll_tables()

    def along_x(c):
        p = [comps[c][NY * a : NY * (a + 1)] for a in range(4)]
        out0 = m[0, 1] * p[1] + m[0, 2] * p[2] + m[0, 3] * p[3]
        if ex > 0:
            out0 = out0 - LIFT * src[c, r0 - NY : r0, :]
        out1 = m[1, 0] * p[0] + m[1, 2] * p[2] + m[1, 3] * p[3]
        out2 = m[2, 0] * p[0] + m[2, 1] * p[1] + m[2, 3] * p[3]
        out3 = m[3, 0] * p[0] + m[3, 1] * p[1] + m[3, 2] * p[2]
        if ex < EX - 1:
            out3 = out3 + LIFT * src[c, r0 + CHUNK : r0 + CHUNK + NY, :]
        return jnp.concatenate([out0, out1, out2, out3], axis=0)

    dx_y, dx_z = along_x(1), along_x(2)
    return dy_z - dz_y, dz_x - dx_z, dx_y - dy_x


LOW, HIGH = 0, 1
SIDES = (LOW, HIGH)
FIRST_X = slice(0, NY)
LAST_X = slice(ROWS - NY, ROWS)
X_FACE = (FIRST_X, LAST_X)
Y_FACE = (pl.ds(0, NX, stride=NY), pl.ds(NY - 1, NX, stride=NY))
CORNER = ((0, NY - 1), (ROWS - NY, ROWS - 1))
FACE = (-LIFT, LIFT)
F, A, B = 0, 1, 2


def chunks():
    return [(ex, slice(CHUNK * ex, CHUNK * (ex + 1))) for ex in range(EX)]


def add_faces(xr, yr, field, factor):
    for s in SIDES:
        f = factor(X_FACE[s]) * FACE[s]
        field[1, X_FACE[s], :] -= f * xr[s, 1]
        field[2, X_FACE[s], :] += f * xr[s, 0]
    for s in SIDES:
        f = factor(Y_FACE[s]) * FACE[s]
        field[0, Y_FACE[s], :] += f * yr[s, 1]
        field[2, Y_FACE[s], :] -= f * yr[s, 0]


def complete_faces(xr, yr, corners, field, factor):
    for s in SIDES:
        f = -FACE[s] * factor
        xr[s, 0] -= f * field[2, X_FACE[s], :]
        xr[s, 1] += f * field[1, X_FACE[s], :]
        xr[s, 1, 0:1, :] -= FACE[LOW] * factor * corners[2 * s + LOW, 0:1, :]
        xr[s, 1, NY - 1 : NY, :] -= FACE[HIGH] * factor * corners[2 * s + HIGH, 0:1, :]
    for s in SIDES:
        f = -FACE[s] * factor
        yr[s, 0] += f * field[2, Y_FACE[s], :]
        yr[s, 1] -= f * field[0, Y_FACE[s], :]
        yr[s, 1, 0:1, :] += FACE[LOW] * factor * corners[2 * LOW + s, 1:2, :]
        yr[s, 1, NX - 1 : NX, :] += FACE[HIGH] * factor * corners[2 * HIGH + s, 1:2, :]


def kernel(
    n_gx,
    n_gy,
    e_in, h_in, j_in, le_in, lh_in, lj_in, eps_in, mat_in, blk_in, wz_in, wy_in, wt_in, wm_in,
    oe_out, oh_out, oj_out, grad_ref,
    eb, hb, jb, leb, lhb, ljb, epsb, mat, blk, wz, wy, wt, wm,
    e0, h1, e1, h2, tot1, sc1, mid1, tot0, sc0, mid0, le0, lj1, q,
    step, drude, part, onehot, oeb, ohb, ojb,
    uys, vxs, vys, cs, uxr, uyr, vxr, vyr, cr,
    wxs, wys, wcs, ids, wxr, wyr, wcr, idr,
    gsend, grecv, msend, mrecv,
    in_sem, out_sem, u_send, u_recv, v_send, v_recv, c_send, c_recv,
    w_send, w_recv, i_send, i_recv, g_send_sem, g_recv_sem, m_send_sem, m_recv_sem,
):
    gx, gy = lax.axis_index("gx"), lax.axis_index("gy")
    near_x = (lax.rem(gx + n_gx - 1, n_gx), lax.rem(gx + 1, n_gx))
    near_y = (lax.rem(gy + n_gy - 1, n_gy), lax.rem(gy + 1, n_gy))

    def load(index, src, dst):
        copy = pltpu.make_async_copy(src, dst, in_sem.at[index])
        copy.start()
        return copy

    in_e = load(0, e_in, eb)
    in_h = load(7, h_in, hb)
    in_wz = load(5, wz_in, wz)
    in_wy = load(6, wy_in, wy)

    barrier = pltpu.get_barrier_semaphore()
    peers = [(near_x[a], near_y[b]) for a in SIDES for b in SIDES]
    peers += [(lax.rem(gx + k, n_gx), gy) for k in range(1, n_gx)]
    peers += [(gx, lax.rem(gy + k, n_gy)) for k in range(1, n_gy)]
    for peer in peers:
        pl.semaphore_signal(barrier, inc=1, device_id=peer, device_id_type=MESH)

    in_le = load(1, le_in, leb)
    in_lj = load(2, lj_in, ljb)
    in_eps = load(3, eps_in, epsb)
    in_mat = load(4, mat_in, mat)
    in_lh = load(8, lh_in, lhb)
    in_j = load(9, j_in, jb)
    in_blk = load(10, blk_in, blk)
    in_wt = load(11, wt_in, wt)
    in_wm = load(12, wm_in, wm)

    started = []

    def remote(src, dst, send_sem, recv_sem, target):
        copy = pltpu.make_async_remote_copy(
            src_ref=src, dst_ref=dst, send_sem=send_sem, recv_sem=recv_sem,
            device_id=target, device_id_type=MESH,
        )
        copy.start()
        started.append(copy)
        return copy

    def stage_u(k, field):
        for s in SIDES:
            uys[k, s, 0] = field[0, Y_FACE[s], :]
            uys[k, s, 1] = field[2, Y_FACE[s], :]
            for t in SIDES:
                row = CORNER[s][t]
                cs[k, 2 * s + t, 0:1, :] = field[0, row : row + 1, :]
                cs[k, 2 * s + t, 1:2, :] = field[1, row : row + 1, :]

    def stage_v(k, field):
        for s in SIDES:
            vxs[k, s, 0] = field[1, X_FACE[s], :]
            vxs[k, s, 1] = field[2, X_FACE[s], :]
            vys[k, s, 0] = field[0, Y_FACE[s], :]
            vys[k, s, 1] = field[2, Y_FACE[s], :]

    def send_u(k, field):
        copies = []
        for s in SIDES:
            src = field.at[pl.ds(1, 2), pl.ds(s * (ROWS - NY), NY)]
            copies.append(
                remote(src, uxr.at[k, 1 - s], u_send.at[k, s], u_recv.at[k, s], (near_x[s], gy))
            )
        for s in SIDES:
            copies.append(
                remote(
                    uys.at[k, s], uyr.at[k, 1 - s], u_send.at[k, 2 + s], u_recv.at[k, 2 + s],
                    (gx, near_y[s]),
                )
            )
        return copies

    def send_corners(k):
        return [
            remote(
                cs.at[k, 2 * s + t], cr.at[k, 2 * (1 - s) + 1 - t],
                c_send.at[k, 2 * s + t], c_recv.at[k, 2 * s + t], (near_x[s], near_y[t]),
            )
            for s in SIDES
            for t in SIDES
        ]

    def send_v(k):
        copies = []
        for s in SIDES:
            copies.append(
                remote(
                    vxs.at[k, s], vxr.at[k, 1 - s], v_send.at[k, s], v_recv.at[k, s],
                    (near_x[s], gy),
                )
            )
        for s in SIDES:
            copies.append(
                remote(
                    vys.at[k, s], vyr.at[k, 1 - s], v_send.at[k, 2 + s], v_recv.at[k, 2 + s],
                    (gx, near_y[s]),
                )
            )
        return copies

    def arrived(copies):
        for copy in copies:
            copy.wait_recv()

    by_step = lambda rows: step[rows, :]
    by_dt = lambda rows: -DT
    by_one = lambda rows: 1.0
    by_step_dt = lambda rows: -DT * step[rows, :]

    in_e.wait()
    for c in range(3):
        e0[c] = eb[c].astype(F32)
    in_wz.wait()
    in_wy.wait()
    in_h.wait()
    for ex, rows in chunks():
        curl = curl_chunk(e0, ex, wz, wy, exact=True)
        for c in range(3):
            h1[c, rows, :] = hb[c, rows, :].astype(F32) - DT * curl[c]
    stage_u(F, e0)
    stage_v(F, h1)

    in_mat.wait()
    in_eps.wait()
    zpick = (
        lax.broadcasted_iota(jnp.int32, (EZ, NZ), 0) == lax.broadcasted_iota(jnp.int32, (EZ, NZ), 1) >> 2
    ).astype(F32).astype(BF16)
    ypick = (
        lax.broadcasted_iota(jnp.int32, (NY, EY), 0) >> 2 == lax.broadcasted_iota(jnp.int32, (NY, EY), 1)
    ).astype(F32).astype(BF16)
    for ex, rows in chunks():
        picked = jnp.dot(mat[ex].astype(F32).astype(BF16), zpick, preferred_element_type=F32)
        plane = jnp.dot(ypick, picked.astype(BF16), preferred_element_type=F32)
        for a in range(4):
            drude[CHUNK * ex + NY * a : CHUNK * ex + NY * (a + 1), :] = plane
    step[...] = DT / epsb[...].astype(F32)
    in_le.wait()
    in_lj.wait()
    for c in range(3):
        total = leb[c].astype(F32) + PDT * drude[...] * ljb[c].astype(F32)
        tot1[c] = total
        sc1[c] = step[...] * total
    in_lh.wait()
    for ex, rows in chunks():
        curl = curl_chunk(sc1, ex, wz, wy)
        for c in range(3):
            mid1[c, rows, :] = lhb[c, rows, :].astype(F32) + curl[c]
    stage_u(A, sc1)
    stage_v(A, mid1)

    pl.semaphore_wait(barrier, len(peers))
    fu = send_u(F, e0)
    fv = send_v(F)
    fc = send_corners(F)
    au = send_u(A, sc1)
    av = send_v(A)
    ac = send_corners(A)

    for c in range(3):
        q[c] = sc1[c] * step[...]
    m = 2.0 * gll_tables()
    w4 = (1.0, 5.0, 5.0, 1.0)
    for s in SIDES:
        end = 3 * s
        for c in range(3):
            wxs[s, c] = q[c, X_FACE[s], :]
            wys[s, c] = q[c, Y_FACE[s], :]
        inner = [a for a in range(4) if a != end]
        for slot, c in ((3, 1), (4, 2)):
            acc = None
            for a in inner:
                r0 = NY * ((NX - 4) * s + a)
                term = (m[a, end] * w4[a]) * q[c, r0 : r0 + NY, :]
                acc = term if acc is None else acc + term
            wxs[s, slot] = acc
        for slot, c in ((3, 0), (4, 2)):
            acc = None
            for a in inner:
                term = (m[a, end] * w4[a]) * q[c, pl.ds((NY - 4) * s + a, NX, stride=NY), :]
                acc = term if acc is None else acc + term
            wys[s, slot] = acc
        for t in SIDES:
            row = CORNER[s][t]
            wcs[2 * s + t, 0:1, :] = q[0, row : row + 1, :]
            wcs[2 * s + t, 1:2, :] = q[1, row : row + 1, :]
    in_blk.wait()
    ids[...] = jnp.zeros_like(ids)
    for s in SIDES:
        ids[s, 0:EY, 0:EZ] = blk[(EX - 1) * s]
        for ex in range(EX):
            ids[2 + s, ex : ex + 1, 0:EZ] = blk[ex, (EY - 1) * s : (EY - 1) * s + 1, :]
        for t in SIDES:
            ids[4 + 2 * s + t, 0:1, 0:EZ] = blk[(EX - 1) * s, (EY - 1) * t : (EY - 1) * t + 1, :]
    ws = []
    for s in SIDES:
        to_x, to_y = (near_x[s], gy), (gx, near_y[s])
        ws.append(remote(wxs.at[s], wxr.at[1 - s], w_send.at[s], w_recv.at[s], to_x))
        ws.append(remote(ids.at[s], idr.at[1 - s], i_send.at[s], i_recv.at[s], to_x))
        ws.append(remote(wys.at[s], wyr.at[1 - s], w_send.at[2 + s], w_recv.at[2 + s], to_y))
        ws.append(remote(ids.at[2 + s], idr.at[3 - s], i_send.at[2 + s], i_recv.at[2 + s], to_y))
        for t in SIDES:
            here, there = 2 * s + t, 2 * (1 - s) + 1 - t
            to = (near_x[s], near_y[t])
            ws.append(remote(wcs.at[here], wcr.at[there], w_send.at[4 + here], w_recv.at[4 + here], to))
            ws.append(
                remote(ids.at[4 + here], idr.at[4 + there], i_send.at[4 + here], i_recv.at[4 + here], to)
            )

    n_rows = gsend.shape[0]
    eye = lax.broadcasted_iota(jnp.int32, (EZ, EZ), 0) == lax.broadcasted_iota(jnp.int32, (EZ, EZ), 1)
    ones = jnp.ones((EZ, 128), BF16)

    def mark(at, rows):
        coarse = jnp.concatenate(
            [jnp.where(eye, (r & -16).astype(F32), 0.0) for r in rows], axis=0
        ).astype(BF16)
        fine = jnp.concatenate(
            [jnp.where(eye, (r & 15).astype(F32), 0.0) for r in rows], axis=0
        ).astype(BF16)
        column = jnp.dot(coarse, ones, preferred_element_type=F32) + jnp.dot(
            fine, ones, preferred_element_type=F32
        )
        column = column.astype(jnp.int32)
        lane = lax.broadcasted_iota(jnp.int32, column.shape, 1)
        for n in range(n_rows):
            onehot[at : at + EZ * len(rows), 128 * n : 128 * (n + 1)] = (
                (column == lane + 128 * n).astype(F32).astype(BF16)
            )

    layer_len = EY * EZ
    for ex in range(EX):
        mark(layer_len * ex, [blk[ex, ey : ey + 1, :] for ey in range(EY)])
    x_at = layer_len * EX
    y_at = x_at + 2 * layer_len
    c_at = y_at + 2 * EX * EZ

    in_j.wait()
    arrived(fu)
    add_faces(uxr.at[F], uyr.at[F], h1, by_dt)
    for ex, rows in chunks():
        curl = curl_chunk(h1, ex, wz, wy)
        for c in range(3):
            e1[c, rows, :] = e0[c, rows, :] + step[rows, :] * (
                curl[c] - drude[rows, :] * jb[c, rows, :].astype(F32)
            )
    arrived(fv)
    arrived(fc)
    complete_faces(vxr.at[F], vyr.at[F], cr.at[F], e0, -DT)
    add_faces(vxr.at[F], vyr.at[F], e1, by_step)

    arrived(au)
    add_faces(uxr.at[A], uyr.at[A], mid1, by_one)
    for ex, rows in chunks():
        curl = curl_chunk(mid1, ex, wz, wy)
        for c in range(3):
            lj = drude[rows, :] * (DECAY * ljb[c, rows, :].astype(F32) - sc1[c, rows, :])
            lj1[c, rows, :] = lj
            total = tot1[c, rows, :] - DT * curl[c] + PDT * lj
            tot0[c, rows, :] = total
            sc0[c, rows, :] = step[rows, :] * total
    arrived(av)
    arrived(ac)
    complete_faces(vxr.at[A], vyr.at[A], cr.at[A], sc1, 1.0)
    add_faces(vxr.at[A], vyr.at[A], tot0, by_dt)
    add_faces(vxr.at[A], vyr.at[A], sc0, by_step_dt)
    stage_u(B, sc0)
    bu = send_u(B, sc0)
    bc = send_corners(B)
    for ex, rows in chunks():
        curl = curl_chunk(sc0, ex, wz, wy)
        for c in range(3):
            mid0[c, rows, :] = mid1[c, rows, :] + curl[c]
    stage_v(B, mid0)
    bv = send_v(B)

    for ex, rows in chunks():
        curl = curl_chunk(e1, ex, wz, wy)
        for c in range(3):
            h2[c, rows, :] = h1[c, rows, :] - DT * curl[c]
    for ex, rows in chunks():
        curl = curl_chunk(h2, ex, wz, wy)
        node, early = None, None
        for c in range(3):
            current = drude[rows, :] * (DECAY * jb[c, rows, :].astype(F32) + PDT * e1[c, rows, :])
            term = q[c, rows, :] * (curl[c] - current)
            node = term if node is None else node + term
            term = tot0[c, rows, :] * (e1[c, rows, :] - e0[c, rows, :])
            early = term if early is None else early + term
        part[rows, :] = node + step[rows, :] * early
    back = LIFT * LIFT * DT
    for s in SIDES:
        x, y = X_FACE[s], Y_FACE[s]
        part[x, :] -= back * (q[1, x, :] * e1[1, x, :] + q[2, x, :] * e1[2, x, :])
        part[y, :] -= back * (q[0, y, :] * e1[0, y, :] + q[2, y, :] * e1[2, y, :])

    arrived(ws)
    mark(x_at, [idr[s, ey : ey + 1, 0:EZ] for s in SIDES for ey in range(EY)])
    mark(y_at, [idr[2 + s, ex : ex + 1, 0:EZ] for s in SIDES for ex in range(EX)])
    mark(c_at, [idr[4 + k, 0:1, 0:EZ] for k in range(4)])
    xa = [-FACE[s] * DT * e1[2, X_FACE[s], :] for s in SIDES]
    xb = [FACE[s] * DT * e1[1, X_FACE[s], :] for s in SIDES]
    ya = [FACE[s] * DT * e1[2, Y_FACE[s], :] for s in SIDES]
    yb = [-FACE[s] * DT * e1[0, Y_FACE[s], :] for s in SIDES]

    def along_z(value):
        high, low = split(value)
        out = jnp.dot(jnp.concatenate([high, low], axis=1), wz[...], preferred_element_type=F32)
        return out[:, 0:NZ] + out[:, NZ : 2 * NZ]

    def along_rows(values):
        n = values[0].shape[0]
        high, low = split(jnp.concatenate(values, axis=1))
        top, rest = wy[0:n, 0:n], wy[CHUNK : CHUNK + n, 0:n]
        out = (
            jnp.dot(top, high, preferred_element_type=F32)
            + jnp.dot(top, low, preferred_element_type=F32)
            + jnp.dot(rest, high, preferred_element_type=F32)
        )
        return out[:, 0:NZ], out[:, NZ : 2 * NZ]

    xaz, yaz = [along_z(v) for v in xa], [along_z(v) for v in ya]
    xby, ybx = along_rows(xb), along_rows(yb)
    planes = []
    for s in SIDES:
        w = wxr.at[s]
        hy, hz = h2[1, X_FACE[s], :], h2[2, X_FACE[s], :]
        planes.append(
            w[0] * (xby[s] - xaz[s]) - w[3] * xb[s] + w[4] * xa[s]
            + FACE[s] * (w[1] * hz - w[2] * hy)
        )
    for s in SIDES:
        w = wyr.at[s]
        hx, hz = h2[0, Y_FACE[s], :], h2[2, Y_FACE[s], :]
        planes.append(
            w[1] * (yaz[s] - ybx[s]) + w[3] * yb[s] - w[4] * ya[s]
            + FACE[s] * (w[2] * hx - w[0] * hz)
        )
    for s in SIDES:
        for t in SIDES:
            row = CORNER[s][t]
            planes.append(
                (-FACE[s] * FACE[t] * DT)
                * (
                    wcr[2 * s + t, 1:2, :] * e1[0, row : row + 1, :]
                    + wcr[2 * s + t, 0:1, :] * e1[1, row : row + 1, :]
                )
            )

    in_wt.wait()
    in_wm.wait()
    layers = []
    for ex in range(EX):
        n = [part[CHUNK * ex + NY * a : CHUNK * ex + NY * (a + 1), :] for a in range(4)]
        layers.append(n[0] + n[3] + 5.0 * (n[1] + n[2]))
    scale = -1.0 / (216.0 * 8.0 * DT)

    def by_element(layer, count, weights):
        high, low = split(layer)
        w = wt[:, 0 : count * EZ]
        wide = jnp.dot(high, w, preferred_element_type=F32) + jnp.dot(
            low, w, preferred_element_type=F32
        )
        return jnp.sum(wide * weights, axis=0, keepdims=True) * scale

    def by_block(flat, at):
        n = flat.shape[1]
        row = lax.broadcasted_iota(jnp.int32, (16, n), 0)
        flat = jnp.broadcast_to(flat, (16, n))
        top = flat.astype(BF16).astype(F32)
        mid = (flat - top).astype(BF16).astype(F32)
        pieces = jnp.where(
            row == 0, top, jnp.where(row == 1, mid, jnp.where(row == 2, flat - top - mid, 0.0))
        ).astype(BF16)
        return jnp.dot(pieces, onehot[at : at + n, :], preferred_element_type=F32)

    sums = jnp.zeros((16, 128 * n_rows), F32)
    for i, layer in enumerate(layers + planes[0:2]):
        sums = sums + by_block(by_element(layer, EY, wm[...]), layer_len * i)
    for s in SIDES:
        flat = by_element(planes[2 + s], EX, wm[0:NX, 0 : EX * EZ])
        sums = sums + by_block(flat, y_at + EX * EZ * s)
    for k in range(4):
        flat = by_element(jnp.broadcast_to(planes[4 + k], (8, NZ)), 1, 0.125)
        sums = sums + by_block(flat, c_at + EZ * k)
    total = jnp.sum(sums, axis=0, keepdims=True)
    for n in range(n_rows):
        gsend[n] = total[:, 128 * n : 128 * (n + 1)]
    width = 2 * n_gy
    per_row = 128 // width
    phase1 = []
    for k in range(1, n_gx):
        p = lax.rem(gx + k, n_gx)
        phase1.append(
            remote(
                gsend.at[lax.div(p, per_row)], grecv.at[k], g_send_sem.at[k], g_recv_sem.at[k], (p, gy)
            )
        )

    for c in range(3):
        ojb[c] = (drude[...] * (DECAY * lj1[c] - sc0[c])).astype(BF16)
    out_j = pltpu.make_async_copy(ojb, oj_out, out_sem.at[1])
    out_j.start()

    mine = gsend[lax.div(gx, per_row)]
    arrived(phase1)
    for k in range(1, n_gx):
        mine = mine + grecv[k]
    msend[...] = mine
    phase2 = []
    for k in range(1, n_gy):
        phase2.append(
            remote(
                msend, mrecv.at[k], m_send_sem.at[k], m_recv_sem.at[k], (gx, lax.rem(gy + k, n_gy))
            )
        )

    arrived(bu)
    add_faces(uxr.at[B], uyr.at[B], mid0, by_one)
    for c in range(3):
        ohb[c] = mid0[c].astype(BF16)
    out_h = pltpu.make_async_copy(ohb, oh_out, out_sem.at[0])
    out_h.start()
    for ex, rows in chunks():
        curl = curl_chunk(mid0, ex, wz, wy)
        for c in range(3):
            le0[c, rows, :] = tot0[c, rows, :] - DT * curl[c]
    arrived(bv)
    arrived(bc)
    complete_faces(vxr.at[B], vyr.at[B], cr.at[B], sc0, 1.0)
    add_faces(vxr.at[B], vyr.at[B], le0, by_dt)
    for c in range(3):
        oeb[c] = le0[c].astype(BF16)
    out_e = pltpu.make_async_copy(oeb, oe_out, out_sem.at[2])
    out_e.start()

    for copy in started:
        copy.wait_send()
    out_h.wait()
    out_j.wait()
    out_e.wait()
    arrived(phase2)
    for k in range(1, n_gy):
        mine = mine + mrecv[k]
    at = lax.rem(gx, per_row) * width + 2 * gy
    lanes = lax.broadcasted_iota(jnp.int32, (1, 128), 1)
    first = jnp.sum(jnp.where(lanes == at, mine, 0.0), axis=1, keepdims=True)
    second = jnp.sum(jnp.where(lanes == at + 1, mine, 0.0), axis=1, keepdims=True)
    grad_ref[...] = jnp.where(lanes == 0, first, second)


def per_device(n_gx, n_gy, *args):
    fields = [a.reshape(3, ROWS, NZ) for a in args[0:6]]
    eps = args[6].reshape(ROWS, NZ)
    blocks = EX * n_gx // CB * (EY * n_gy // CB)
    n_rows = -(-blocks // 128)
    consts = [jnp.asarray(a) for a in constant_arrays()]
    hbm = pl.BlockSpec(memory_space=pl.ANY)
    field32 = pltpu.VMEM((3, ROWS, NZ), F32)
    field16 = pltpu.VMEM((3, ROWS, NZ), BF16)
    plane32 = pltpu.VMEM((ROWS, NZ), F32)
    out16 = jax.ShapeDtypeStruct((3, ROWS, NZ), BF16)
    dma = pltpu.SemaphoreType.DMA
    x_faces = pltpu.VMEM((3, 2, 2, NY, NZ), F32)
    y_faces = pltpu.VMEM((3, 2, 2, NX, NZ), F32)
    corners = pltpu.VMEM((3, 4, 2, NZ), F32)
    weights = [
        pltpu.VMEM((2, 5, NY, NZ), F32),
        pltpu.VMEM((2, 5, NX, NZ), F32),
        pltpu.VMEM((4, 2, NZ), F32),
        pltpu.VMEM((8, 8, 128), jnp.int32),
    ]
    marked = EX * EY * EZ + 2 * EY * EZ + 2 * EX * EZ + 4 * EZ
    oe, oh, oj, grad = pl.pallas_call(
        functools.partial(kernel, n_gx, n_gy),
        out_shape=(out16, out16, out16, jax.ShapeDtypeStruct((1, 128), F32)),
        in_specs=[hbm] * 13,
        out_specs=(hbm, hbm, hbm, pl.BlockSpec(memory_space=pltpu.VMEM)),
        scratch_shapes=[
            *[field16] * 6,
            pltpu.VMEM((ROWS, NZ), BF16),
            pltpu.VMEM((EX, EY, EZ), jnp.int32),
            pltpu.VMEM((EX, EY, EZ), jnp.int32),
            *[pltpu.VMEM(a.shape, a.dtype) for a in consts],
            *[field32] * 13,
            plane32,
            plane32,
            plane32,
            pltpu.VMEM((marked, 128 * n_rows), BF16),
            *[field16] * 3,
            y_faces, x_faces, y_faces, corners,
            x_faces, y_faces, x_faces, y_faces, corners,
            *weights,
            *weights,
            pltpu.VMEM((n_rows, 1, 128), F32),
            pltpu.VMEM((n_gx, 1, 128), F32),
            pltpu.VMEM((1, 128), F32),
            pltpu.VMEM((n_gy, 1, 128), F32),
            dma((13,)), dma((3,)),
            dma((3, 4)), dma((3, 4)), dma((3, 4)), dma((3, 4)), dma((3, 4)), dma((3, 4)),
            dma((8,)), dma((8,)), dma((8,)), dma((8,)),
            dma((n_gx,)), dma((n_gx,)), dma((n_gy,)), dma((n_gy,)),
        ],
        compiler_params=pltpu.CompilerParams(
            collective_id=0, has_side_effects=True, vmem_limit_bytes=60 * 1024 * 1024
        ),
    )(*fields, eps, args[7], args[8], *consts)
    shape = args[0].shape
    return oe.reshape(shape), oh.reshape(shape), oj.reshape(shape), grad[0, 0:2]


def solution(mesh):
    n_gx, n_gy = mesh.shape["gx"], mesh.shape["gy"]
    field = P(None, "gx", "gy", None)
    node = P("gx", "gy", None)
    return jax.shard_map(
        functools.partial(per_device, n_gx, n_gy),
        mesh=mesh,
        in_specs=(field,) * 6 + (node,) * 3,
        out_specs=(field, field, field, P(("gx", "gy"))),
        check_vma=False,
    )
```

time: 58.8 us -> 42.3 us (0.72)
  local copies, waits for them, and re-layouts: 13.8 us -> 4.56 us
  Pallas kernels: 43.7 us -> 36.9 us
    unnamed x29 -> x9, local copies, waits for them, and re-layouts: 13.3 us -> 4.04 us
    pallas_call x1, Pallas kernels: 43.7 us -> 36.9 us  [per_device(): pl.pallas_call(functools.partial(kernel, n_gx, n_gy), out_shape=(out16, o...]
where the time goes in v1:
time: 42.3 us; the launch traced here: 42.1 us
  Pallas kernels  36.9 us (87%)
  local copies, waits for them, and re-layouts  4.56 us (11%)
  between operations  0.65 us (2%)
    pallas_call x1, Pallas kernels, per_device(): pl.pallas_call(functools.partial(kernel, n_gx, n_gy), out_shape=(out16, o...  36.9 us
    unnamed x9, local copies, waits for them, and re-layouts  4.04 us

profile of v1, /device:TPU:1, one launch (start us, length us, event | category | flops | bytes accessed | tf_op | source)
XLA Modules:
  0.0 42.1 jit_solution(7987943768416105256)
XLA Ops:
  0.6 36.9 %shard_map.156 = (bf16[3,288,128]{2,1,0:T(8,128)(2,1)}, bf16[3,288,128]{2,1,0:T(8,128)(2,1)}, bf16[3,288,128]{2,1,0:T(8,128)(2,1)}, f32[1,128]{1,0:T(1,128)}) custom-call(bf16[3,288,128]{2,1,0:T(8,128)(2,1)} %bitcast.15, bf16[3,288,128]{2,1,0:T(8,128)(2,1)} %bitcast.16, bf16[3,288,128]{2,1,0:T(8,128)(2,1)} %bitcast.17, bf16[3,288,128]{2,1,0:T(8,128)(2,1)} %bitcast.18, ...), custom_call_target="tpu_custom_call" | custom-call | tf_op jit(solution)/shard_map/pallas_call | solution.py:660
  37.6 0.0 copy-start.2
  37.6 0.7 %copy-done.2 = f32[1,128]{1,0:T(1,128)S(1)} copy-done((f32[1,128]{1,0:T(1,128)S(1)}, f32[1,128]{1,0:T(1,128)}, u32[]{:S(2)}) %copy-start.2) | copy-done | bytes 536
  38.2 0.5 %slice_bitcast_fusion = f32[2]{0:T(128)} fusion(f32[1,128]{1,0:T(1,128)S(1)} %copy-done.2), kind=kLoop, calls=%fused_computation | loop fusion | bytes 16 | tf_op jit(solution)/shard_map/squeeze | solution.py:695
  38.7 0.0 copy-start.1
  38.7 1.7 %copy.20 = bf16[3,12,24,128]{3,2,1,0:T(8,128)(2,1)} copy(bf16[3,12,24,128]{3,2,1,0:T(8,128)(2,1)} %bitcast.14) | data formatting | bytes 442368
  40.4 0.0 copy-done.1
  40.4 0.0 copy-start
  40.4 0.7 %copy.21 = bf16[3,12,24,128]{3,2,1,0:T(8,128)(2,1)} copy(bf16[3,12,24,128]{3,2,1,0:T(8,128)(2,1)S(1)} %bitcast.13) | data formatting | bytes 442368
  41.1 0.3 copy-done
  41.4 0.7 %copy.22 = bf16[3,12,24,128]{3,2,1,0:T(8,128)(2,1)} copy(bf16[3,12,24,128]{3,2,1,0:T(8,128)(2,1)S(1)} %bitcast.12) | data formatting | bytes 442368
Async XLA Ops:
  37.6 0.7 %copy-start.2 = (f32[1,128]{1,0:T(1,128)S(1)}, f32[1,128]{1,0:T(1,128)}, u32[]{:S(2)}) copy-start(f32[1,128]{1,0:T(1,128)} %get-tuple-element.11) | copy-start | bytes 1540
  38.7 1.7 %copy-start.1 = (bf16[3,288,128]{2,1,0:T(8,128)(2,1)S(1)}, bf16[3,288,128]{2,1,0:T(8,128)(2,1)}, u32[]{:S(2)}) copy-start(bf16[3,288,128]{2,1,0:T(8,128)(2,1)} %get-tuple-element.9) | copy-start | bytes 663556
  40.4 1.0 %copy-start = (bf16[3,288,128]{2,1,0:T(8,128)(2,1)S(1)}, bf16[3,288,128]{2,1,0:T(8,128)(2,1)}, u32[]{:S(2)}) copy-start(bf16[3,288,128]{2,1,0:T(8,128)(2,1)} %get-tuple-element.10) | copy-start | bytes 663556

commit v2 on v1

--- a/solution.py
+++ b/solution.py
@@ -176,11 +176,11 @@
     oe_out, oh_out, oj_out, grad_ref,
     eb, hb, jb, leb, lhb, ljb, epsb, mat, blk, wz, wy, wt, wm,
     e0, h1, e1, h2, tot1, sc1, mid1, tot0, sc0, mid0, le0, lj1, q,
-    step, drude, part, onehot, oeb, ohb, ojb,
+    step, drude, part, onehot,
     uys, vxs, vys, cs, uxr, uyr, vxr, vyr, cr,
     wxs, wys, wcs, ids, wxr, wyr, wcr, idr,
     gsend, grecv, msend, mrecv,
-    in_sem, out_sem, u_send, u_recv, v_send, v_recv, c_send, c_recv,
+    in_sem, u_send, u_recv, v_send, v_recv, c_send, c_recv,
     w_send, w_recv, i_send, i_recv, g_send_sem, g_recv_sem, m_send_sem, m_recv_sem,
 ):
     gx, gy = lax.axis_index("gx"), lax.axis_index("gy")
@@ -335,6 +335,14 @@
     stage_u(A, sc1)
     stage_v(A, mid1)
 
+    in_blk.wait()
+    ids[...] = jnp.zeros_like(ids)
+    for s in SIDES:
+        ids[s, 0:EY, 0:EZ] = blk[(EX - 1) * s]
+        for ex in range(EX):
+            ids[2 + s, ex : ex + 1, 0:EZ] = blk[ex, (EY - 1) * s : (EY - 1) * s + 1, :]
+        for t in SIDES:
+            ids[4 + 2 * s + t, 0:1, 0:EZ] = blk[(EX - 1) * s, (EY - 1) * t : (EY - 1) * t + 1, :]
     pl.semaphore_wait(barrier, len(peers))
     fu = send_u(F, e0)
     fv = send_v(F)
@@ -342,6 +350,20 @@
     au = send_u(A, sc1)
     av = send_v(A)
     ac = send_corners(A)
+    marks = []
+    for s in SIDES:
+        marks.append(remote(ids.at[s], idr.at[1 - s], i_send.at[s], i_recv.at[s], (near_x[s], gy)))
+        marks.append(
+            remote(ids.at[2 + s], idr.at[3 - s], i_send.at[2 + s], i_recv.at[2 + s], (gx, near_y[s]))
+        )
+        for t in SIDES:
+            here, there = 4 + 2 * s + t, 4 + 2 * (1 - s) + 1 - t
+            marks.append(
+                remote(
+                    ids.at[here], idr.at[there], i_send.at[here], i_recv.at[here],
+                    (near_x[s], near_y[t]),
+                )
+            )
 
     for c in range(3):
         q[c] = sc1[c] * step[...]
@@ -349,18 +371,19 @@
     w4 = (1.0, 5.0, 5.0, 1.0)
     for s in SIDES:
         end = 3 * s
-        for c in range(3):
-            wxs[s, c] = q[c, X_FACE[s], :]
-            wys[s, c] = q[c, Y_FACE[s], :]
+        wxs[s, 0] = step[X_FACE[s], :]
+        wxs[s, 1] = q[0, X_FACE[s], :]
+        wys[s, 0] = step[Y_FACE[s], :]
+        wys[s, 1] = q[1, Y_FACE[s], :]
         inner = [a for a in range(4) if a != end]
-        for slot, c in ((3, 1), (4, 2)):
+        for slot, c in ((2, 1), (3, 2)):
             acc = None
             for a in inner:
                 r0 = NY * ((NX - 4) * s + a)
                 term = (m[a, end] * w4[a]) * q[c, r0 : r0 + NY, :]
                 acc = term if acc is None else acc + term
             wxs[s, slot] = acc
-        for slot, c in ((3, 0), (4, 2)):
+        for slot, c in ((2, 0), (3, 2)):
             acc = None
             for a in inner:
                 term = (m[a, end] * w4[a]) * q[c, pl.ds((NY - 4) * s + a, NX, stride=NY), :]
@@ -370,28 +393,15 @@
             row = CORNER[s][t]
             wcs[2 * s + t, 0:1, :] = q[0, row : row + 1, :]
             wcs[2 * s + t, 1:2, :] = q[1, row : row + 1, :]
-    in_blk.wait()
-    ids[...] = jnp.zeros_like(ids)
-    for s in SIDES:
-        ids[s, 0:EY, 0:EZ] = blk[(EX - 1) * s]
-        for ex in range(EX):
-            ids[2 + s, ex : ex + 1, 0:EZ] = blk[ex, (EY - 1) * s : (EY - 1) * s + 1, :]
-        for t in SIDES:
-            ids[4 + 2 * s + t, 0:1, 0:EZ] = blk[(EX - 1) * s, (EY - 1) * t : (EY - 1) * t + 1, :]
     ws = []
     for s in SIDES:
         to_x, to_y = (near_x[s], gy), (gx, near_y[s])
         ws.append(remote(wxs.at[s], wxr.at[1 - s], w_send.at[s], w_recv.at[s], to_x))
-        ws.append(remote(ids.at[s], idr.at[1 - s], i_send.at[s], i_recv.at[s], to_x))
         ws.append(remote(wys.at[s], wyr.at[1 - s], w_send.at[2 + s], w_recv.at[2 + s], to_y))
-        ws.append(remote(ids.at[2 + s], idr.at[3 - s], i_send.at[2 + s], i_recv.at[2 + s], to_y))
         for t in SIDES:
             here, there = 2 * s + t, 2 * (1 - s) + 1 - t
             to = (near_x[s], near_y[t])
             ws.append(remote(wcs.at[here], wcr.at[there], w_send.at[4 + here], w_recv.at[4 + here], to))
-            ws.append(
-                remote(ids.at[4 + here], idr.at[4 + there], i_send.at[4 + here], i_recv.at[4 + here], to)
-            )
 
     n_rows = gsend.shape[0]
     eye = lax.broadcasted_iota(jnp.int32, (EZ, EZ), 0) == lax.broadcasted_iota(jnp.int32, (EZ, EZ), 1)
@@ -480,7 +490,7 @@
         part[x, :] -= back * (q[1, x, :] * e1[1, x, :] + q[2, x, :] * e1[2, x, :])
         part[y, :] -= back * (q[0, y, :] * e1[0, y, :] + q[2, y, :] * e1[2, y, :])
 
-    arrived(ws)
+    arrived(marks)
     mark(x_at, [idr[s, ey : ey + 1, 0:EZ] for s in SIDES for ey in range(EY)])
     mark(y_at, [idr[2 + s, ex : ex + 1, 0:EZ] for s in SIDES for ex in range(EX)])
     mark(c_at, [idr[4 + k, 0:1, 0:EZ] for k in range(4)])
@@ -507,32 +517,6 @@
 
     xaz, yaz = [along_z(v) for v in xa], [along_z(v) for v in ya]
     xby, ybx = along_rows(xb), along_rows(yb)
-    planes = []
-    for s in SIDES:
-        w = wxr.at[s]
-        hy, hz = h2[1, X_FACE[s], :], h2[2, X_FACE[s], :]
-        planes.append(
-            w[0] * (xby[s] - xaz[s]) - w[3] * xb[s] + w[4] * xa[s]
-            + FACE[s] * (w[1] * hz - w[2] * hy)
-        )
-    for s in SIDES:
-        w = wyr.at[s]
-        hx, hz = h2[0, Y_FACE[s], :], h2[2, Y_FACE[s], :]
-        planes.append(
-            w[1] * (yaz[s] - ybx[s]) + w[3] * yb[s] - w[4] * ya[s]
-            + FACE[s] * (w[2] * hx - w[0] * hz)
-        )
-    for s in SIDES:
-        for t in SIDES:
-            row = CORNER[s][t]
-            planes.append(
-                (-FACE[s] * FACE[t] * DT)
-                * (
-                    wcr[2 * s + t, 1:2, :] * e1[0, row : row + 1, :]
-                    + wcr[2 * s + t, 0:1, :] * e1[1, row : row + 1, :]
-                )
-            )
-
     in_wt.wait()
     in_wm.wait()
     layers = []
@@ -561,8 +545,38 @@
         return jnp.dot(pieces, onehot[at : at + n, :], preferred_element_type=F32)
 
     sums = jnp.zeros((16, 128 * n_rows), F32)
-    for i, layer in enumerate(layers + planes[0:2]):
+    for i, layer in enumerate(layers):
         sums = sums + by_block(by_element(layer, EY, wm[...]), layer_len * i)
+
+    arrived(ws)
+    planes = []
+    for s in SIDES:
+        w = wxr.at[s]
+        hy, hz = h2[1, X_FACE[s], :], h2[2, X_FACE[s], :]
+        planes.append(
+            w[1] * (xby[s] - xaz[s]) - w[2] * xb[s] + w[3] * xa[s]
+            + FACE[s] * w[0] * (uxr[A, s, 0] * hz - uxr[A, s, 1] * hy)
+        )
+    for s in SIDES:
+        w = wyr.at[s]
+        hx, hz = h2[0, Y_FACE[s], :], h2[2, Y_FACE[s], :]
+        planes.append(
+            w[1] * (yaz[s] - ybx[s]) + w[2] * yb[s] - w[3] * ya[s]
+            + FACE[s] * w[0] * (uyr[A, s, 1] * hx - uyr[A, s, 0] * hz)
+        )
+    for s in SIDES:
+        for t in SIDES:
+            row = CORNER[s][t]
+            planes.append(
+                (-FACE[s] * FACE[t] * DT)
+                * (
+                    wcr[2 * s + t, 1:2, :] * e1[0, row : row + 1, :]
+                    + wcr[2 * s + t, 0:1, :] * e1[1, row : row + 1, :]
+                )
+            )
+
+    for s in SIDES:
+        sums = sums + by_block(by_element(planes[s], EY, wm[...]), x_at + layer_len * s)
     for s in SIDES:
         flat = by_element(planes[2 + s], EX, wm[0:NX, 0 : EX * EZ])
         sums = sums + by_block(flat, y_at + EX * EZ * s)
@@ -584,9 +598,7 @@
         )
 
     for c in range(3):
-        ojb[c] = (drude[...] * (DECAY * lj1[c] - sc0[c])).astype(BF16)
-    out_j = pltpu.make_async_copy(ojb, oj_out, out_sem.at[1])
-    out_j.start()
+        oj_out[c] = (drude[...] * (DECAY * lj1[c] - sc0[c])).astype(BF16)
 
     mine = gsend[lax.div(gx, per_row)]
     arrived(phase1)
@@ -604,9 +616,7 @@
     arrived(bu)
     add_faces(uxr.at[B], uyr.at[B], mid0, by_one)
     for c in range(3):
-        ohb[c] = mid0[c].astype(BF16)
-    out_h = pltpu.make_async_copy(ohb, oh_out, out_sem.at[0])
-    out_h.start()
+        oh_out[c] = mid0[c].astype(BF16)
     for ex, rows in chunks():
         curl = curl_chunk(mid0, ex, wz, wy)
         for c in range(3):
@@ -616,15 +626,10 @@
     complete_faces(vxr.at[B], vyr.at[B], cr.at[B], sc0, 1.0)
     add_faces(vxr.at[B], vyr.at[B], le0, by_dt)
     for c in range(3):
-        oeb[c] = le0[c].astype(BF16)
-    out_e = pltpu.make_async_copy(oeb, oe_out, out_sem.at[2])
-    out_e.start()
+        oe_out[c] = le0[c].astype(BF16)
 
     for copy in started:
         copy.wait_send()
-    out_h.wait()
-    out_j.wait()
-    out_e.wait()
     arrived(phase2)
     for k in range(1, n_gy):
         mine = mine + mrecv[k]
@@ -633,6 +638,16 @@
     first = jnp.sum(jnp.where(lanes == at, mine, 0.0), axis=1, keepdims=True)
     second = jnp.sum(jnp.where(lanes == at + 1, mine, 0.0), axis=1, keepdims=True)
     grad_ref[...] = jnp.where(lanes == 0, first, second)
+
+
+def write_out(e_in, h_in, j_in, g_in, e_out, h_out, j_out, g_out, sem):
+    pairs = ((e_in, e_out), (h_in, h_out), (j_in, j_out))
+    copies = [pltpu.make_async_copy(a, b, sem.at[i]) for i, (a, b) in enumerate(pairs)]
+    for copy in copies:
+        copy.start()
+    g_out[...] = g_in[0, 0:2]
+    for copy in copies:
+        copy.wait()
 
 
 def per_device(n_gx, n_gy, *args):
@@ -651,17 +666,17 @@
     y_faces = pltpu.VMEM((3, 2, 2, NX, NZ), F32)
     corners = pltpu.VMEM((3, 4, 2, NZ), F32)
     weights = [
-        pltpu.VMEM((2, 5, NY, NZ), F32),
-        pltpu.VMEM((2, 5, NX, NZ), F32),
+        pltpu.VMEM((2, 4, NY, NZ), F32),
+        pltpu.VMEM((2, 4, NX, NZ), F32),
         pltpu.VMEM((4, 2, NZ), F32),
         pltpu.VMEM((8, 8, 128), jnp.int32),
     ]
     marked = EX * EY * EZ + 2 * EY * EZ + 2 * EX * EZ + 4 * EZ
     oe, oh, oj, grad = pl.pallas_call(
         functools.partial(kernel, n_gx, n_gy),
-        out_shape=(out16, out16, out16, jax.ShapeDtypeStruct((1, 128), F32)),
+        out_shape=(pltpu.VMEM((3, ROWS, NZ), BF16),) * 3 + (pltpu.VMEM((1, 128), F32),),
         in_specs=[hbm] * 13,
-        out_specs=(hbm, hbm, hbm, pl.BlockSpec(memory_space=pltpu.VMEM)),
+        out_specs=(pl.BlockSpec(memory_space=pltpu.VMEM),) * 4,
         scratch_shapes=[
             *[field16] * 6,
             pltpu.VMEM((ROWS, NZ), BF16),
@@ -673,7 +688,6 @@
             plane32,
             plane32,
             pltpu.VMEM((marked, 128 * n_rows), BF16),
-            *[field16] * 3,
             y_faces, x_faces, y_faces, corners,
             x_faces, y_faces, x_faces, y_faces, corners,
             *weights,
@@ -682,7 +696,7 @@
             pltpu.VMEM((n_gx, 1, 128), F32),
             pltpu.VMEM((1, 128), F32),
             pltpu.VMEM((n_gy, 1, 128), F32),
-            dma((13,)), dma((3,)),
+            dma((13,)),
             dma((3, 4)), dma((3, 4)), dma((3, 4)), dma((3, 4)), dma((3, 4)), dma((3, 4)),
             dma((8,)), dma((8,)), dma((8,)), dma((8,)),
             dma((n_gx,)), dma((n_gx,)), dma((n_gy,)), dma((n_gy,)),
@@ -691,8 +705,16 @@
             collective_id=0, has_side_effects=True, vmem_limit_bytes=60 * 1024 * 1024
         ),
     )(*fields, eps, args[7], args[8], *consts)
+    oe, oh, oj, grad = pl.pallas_call(
+        write_out,
+        out_shape=(out16, out16, out16, jax.ShapeDtypeStruct((2,), F32)),
+        in_specs=[pl.BlockSpec(memory_space=pltpu.VMEM)] * 4,
+        out_specs=(hbm, hbm, hbm, pl.BlockSpec(memory_space=pltpu.VMEM)),
+        scratch_shapes=[dma((3,))],
+        compiler_params=pltpu.CompilerParams(vmem_limit_bytes=4 * 1024 * 1024),
+    )(oe, oh, oj, grad)
     shape = args[0].shape
-    return oe.reshape(shape), oh.reshape(shape), oj.reshape(shape), grad[0, 0:2]
+    return oe.reshape(shape), oh.reshape(shape), oj.reshape(shape), grad
 
 
 def solution(mesh):

time: 42.3 us -> 37.3 us (0.88)
  local copies, waits for them, and re-layouts: 4.56 us -> 0 us
    unnamed x9 -> x0, local copies, waits for them, and re-layouts: 4.04 us -> none
    squeeze x1 -> x0, local copies, waits for them, and re-layouts: 0.51 us -> none  [per_device(): grad[0, 0:2]]
    pallas_call x1 -> x2, Pallas kernels: 36.9 us -> 36.5 us  [the longest x1 35.1 us: per_device(): pl.pallas_call(functools.partial(kernel, n_gx, n_gy), out_shape=(pltpu.VM...]
where the time goes in v2:
time: 37.3 us; the launch traced here: 37.2 us
  Pallas kernels  36.5 us (98%)
  between operations  0.64 us (2%)
    pallas_call x1, Pallas kernels, per_device(): pl.pallas_call(functools.partial(kernel, n_gx, n_gy), out_shape=(pltpu.VM...  35.1 us
    pallas_call x1, Pallas kernels, per_device(): pl.pallas_call(write_out, out_shape=(out16, out16, out16, jax.ShapeDtypeS...  1.37 us

profile of v2, /device:TPU:1, one launch (start us, length us, event | category | flops | bytes accessed | tf_op | source)
XLA Modules:
  0.0 37.2 jit_solution(18084937973287734607)
XLA Ops:
  0.6 35.1 %shard_map.156 = (bf16[3,288,128]{2,1,0:T(8,128)(2,1)S(1)}, bf16[3,288,128]{2,1,0:T(8,128)(2,1)S(1)}, bf16[3,288,128]{2,1,0:T(8,128)(2,1)S(1)}, f32[1,128]{1,0:T(1,128)S(1)}) custom-call(bf16[3,288,128]{2,1,0:T(8,128)(2,1)} %bitcast.10, bf16[3,288,128]{2,1,0:T(8,128)(2,1)} %bitcast.11, bf16[3,288,128]{2,1,0:T(8,128)(2,1)} %bitcast.12, ...), custom_call_target="tpu_custom_call" | custom-call | tf_op jit(solution)/shard_map/pallas_call | solution.py:675
  35.8 1.4 %shard_map.157 = (bf16[3,288,128]{2,1,0:T(8,128)(2,1)}, bf16[3,288,128]{2,1,0:T(8,128)(2,1)}, bf16[3,288,128]{2,1,0:T(8,128)(2,1)}, f32[2]{0:T(128)}) custom-call(bf16[3,288,128]{2,1,0:T(8,128)(2,1)S(1)} %get-tuple-element.12.e_in, bf16[3,288,128]{2,1,0:T(8,128)(2,1)S(1)} %get-tuple-element.13.h_in, bf16[3,288,128]{2,1,0:T(8,128)(2,1)S(1)} %get-tuple-element.14.j_in, ...), custom_call_target="tpu_custom_call" | custom-call | tf_op jit(solution)/shard_map/pallas_call | solution.py:708

commit v3 on v2

--- a/solution.py
+++ b/solution.py
@@ -154,19 +154,19 @@
         field[2, Y_FACE[s], :] -= f * yr[s, 0]
 
 
-def complete_faces(xr, yr, corners, field, factor):
+def complete_faces(xr, yr, corners, at, field, factor):
     for s in SIDES:
         f = -FACE[s] * factor
         xr[s, 0] -= f * field[2, X_FACE[s], :]
         xr[s, 1] += f * field[1, X_FACE[s], :]
-        xr[s, 1, 0:1, :] -= FACE[LOW] * factor * corners[2 * s + LOW, 0:1, :]
-        xr[s, 1, NY - 1 : NY, :] -= FACE[HIGH] * factor * corners[2 * s + HIGH, 0:1, :]
+        xr[s, 1, 0:1, :] -= FACE[LOW] * factor * corners[2 * s + LOW, at : at + 1, :]
+        xr[s, 1, NY - 1 : NY, :] -= FACE[HIGH] * factor * corners[2 * s + HIGH, at : at + 1, :]
     for s in SIDES:
         f = -FACE[s] * factor
         yr[s, 0] += f * field[2, Y_FACE[s], :]
         yr[s, 1] -= f * field[0, Y_FACE[s], :]
-        yr[s, 1, 0:1, :] += FACE[LOW] * factor * corners[2 * LOW + s, 1:2, :]
-        yr[s, 1, NX - 1 : NX, :] += FACE[HIGH] * factor * corners[2 * HIGH + s, 1:2, :]
+        yr[s, 1, 0:1, :] += FACE[LOW] * factor * corners[2 * LOW + s, at + 1 : at + 2, :]
+        yr[s, 1, NX - 1 : NX, :] += FACE[HIGH] * factor * corners[2 * HIGH + s, at + 1 : at + 2, :]
 
 
 def kernel(
@@ -176,9 +176,9 @@
     oe_out, oh_out, oj_out, grad_ref,
     eb, hb, jb, leb, lhb, ljb, epsb, mat, blk, wz, wy, wt, wm,
     e0, h1, e1, h2, tot1, sc1, mid1, tot0, sc0, mid0, le0, lj1, q,
-    step, drude, part, onehot,
+    step, drude, part, xt, yt, sums, onehot,
     uys, vxs, vys, cs, uxr, uyr, vxr, vyr, cr,
-    wxs, wys, wcs, ids, wxr, wyr, wcr, idr,
+    wxs, wys, ids, wxr, wyr, idr,
     gsend, grecv, msend, mrecv,
     in_sem, u_send, u_recv, v_send, v_recv, c_send, c_recv,
     w_send, w_recv, i_send, i_recv, g_send_sem, g_recv_sem, m_send_sem, m_recv_sem,
@@ -229,10 +229,13 @@
         for s in SIDES:
             uys[k, s, 0] = field[0, Y_FACE[s], :]
             uys[k, s, 1] = field[2, Y_FACE[s], :]
+
+    def stage_corners(k, at, field):
+        for s in SIDES:
             for t in SIDES:
                 row = CORNER[s][t]
-                cs[k, 2 * s + t, 0:1, :] = field[0, row : row + 1, :]
-                cs[k, 2 * s + t, 1:2, :] = field[1, row : row + 1, :]
+                cs[k, 2 * s + t, at : at + 1, :] = field[0, row : row + 1, :]
+                cs[k, 2 * s + t, at + 1 : at + 2, :] = field[1, row : row + 1, :]
 
     def stage_v(k, field):
         for s in SIDES:
@@ -292,7 +295,6 @@
     by_step = lambda rows: step[rows, :]
     by_dt = lambda rows: -DT
     by_one = lambda rows: 1.0
-    by_step_dt = lambda rows: -DT * step[rows, :]
 
     in_e.wait()
     for c in range(3):
@@ -306,6 +308,8 @@
             h1[c, rows, :] = hb[c, rows, :].astype(F32) - DT * curl[c]
     stage_u(F, e0)
     stage_v(F, h1)
+    cs[...] = jnp.zeros_like(cs)
+    stage_corners(0, 0, e0)
 
     in_mat.wait()
     in_eps.wait()
@@ -334,6 +338,10 @@
             mid1[c, rows, :] = lhb[c, rows, :].astype(F32) + curl[c]
     stage_u(A, sc1)
     stage_v(A, mid1)
+    stage_corners(0, 2, sc1)
+    for c in range(3):
+        q[c] = sc1[c] * step[...]
+    stage_corners(0, 4, q)
 
     in_blk.wait()
     ids[...] = jnp.zeros_like(ids)
@@ -342,31 +350,21 @@
         for ex in range(EX):
             ids[2 + s, ex : ex + 1, 0:EZ] = blk[ex, (EY - 1) * s : (EY - 1) * s + 1, :]
         for t in SIDES:
-            ids[4 + 2 * s + t, 0:1, 0:EZ] = blk[(EX - 1) * s, (EY - 1) * t : (EY - 1) * t + 1, :]
+            line = blk[(EX - 1) * s, (EY - 1) * t : (EY - 1) * t + 1, :]
+            cs[0, 2 * s + t, 6:7, 0:EZ] = line.astype(F32)
     pl.semaphore_wait(barrier, len(peers))
     fu = send_u(F, e0)
     fv = send_v(F)
-    fc = send_corners(F)
+    rc = send_corners(0)
     au = send_u(A, sc1)
     av = send_v(A)
-    ac = send_corners(A)
     marks = []
     for s in SIDES:
         marks.append(remote(ids.at[s], idr.at[1 - s], i_send.at[s], i_recv.at[s], (near_x[s], gy)))
         marks.append(
             remote(ids.at[2 + s], idr.at[3 - s], i_send.at[2 + s], i_recv.at[2 + s], (gx, near_y[s]))
         )
-        for t in SIDES:
-            here, there = 4 + 2 * s + t, 4 + 2 * (1 - s) + 1 - t
-            marks.append(
-                remote(
-                    ids.at[here], idr.at[there], i_send.at[here], i_recv.at[here],
-                    (near_x[s], near_y[t]),
-                )
-            )
-
-    for c in range(3):
-        q[c] = sc1[c] * step[...]
+
     m = 2.0 * gll_tables()
     w4 = (1.0, 5.0, 5.0, 1.0)
     for s in SIDES:
@@ -389,19 +387,11 @@
                 term = (m[a, end] * w4[a]) * q[c, pl.ds((NY - 4) * s + a, NX, stride=NY), :]
                 acc = term if acc is None else acc + term
             wys[s, slot] = acc
-        for t in SIDES:
-            row = CORNER[s][t]
-            wcs[2 * s + t, 0:1, :] = q[0, row : row + 1, :]
-            wcs[2 * s + t, 1:2, :] = q[1, row : row + 1, :]
     ws = []
     for s in SIDES:
         to_x, to_y = (near_x[s], gy), (gx, near_y[s])
         ws.append(remote(wxs.at[s], wxr.at[1 - s], w_send.at[s], w_recv.at[s], to_x))
         ws.append(remote(wys.at[s], wyr.at[1 - s], w_send.at[2 + s], w_recv.at[2 + s], to_y))
-        for t in SIDES:
-            here, there = 2 * s + t, 2 * (1 - s) + 1 - t
-            to = (near_x[s], near_y[t])
-            ws.append(remote(wcs.at[here], wcr.at[there], w_send.at[4 + here], w_recv.at[4 + here], to))
 
     n_rows = gsend.shape[0]
     eye = lax.broadcasted_iota(jnp.int32, (EZ, EZ), 0) == lax.broadcasted_iota(jnp.int32, (EZ, EZ), 1)
@@ -441,8 +431,8 @@
                 curl[c] - drude[rows, :] * jb[c, rows, :].astype(F32)
             )
     arrived(fv)
-    arrived(fc)
-    complete_faces(vxr.at[F], vyr.at[F], cr.at[F], e0, -DT)
+    arrived(rc)
+    complete_faces(vxr.at[F], vyr.at[F], cr.at[0], 0, e0, -DT)
     add_faces(vxr.at[F], vyr.at[F], e1, by_step)
 
     arrived(au)
@@ -452,23 +442,7 @@
         for c in range(3):
             lj = drude[rows, :] * (DECAY * ljb[c, rows, :].astype(F32) - sc1[c, rows, :])
             lj1[c, rows, :] = lj
-            total = tot1[c, rows, :] - DT * curl[c] + PDT * lj
-            tot0[c, rows, :] = total
-            sc0[c, rows, :] = step[rows, :] * total
-    arrived(av)
-    arrived(ac)
-    complete_faces(vxr.at[A], vyr.at[A], cr.at[A], sc1, 1.0)
-    add_faces(vxr.at[A], vyr.at[A], tot0, by_dt)
-    add_faces(vxr.at[A], vyr.at[A], sc0, by_step_dt)
-    stage_u(B, sc0)
-    bu = send_u(B, sc0)
-    bc = send_corners(B)
-    for ex, rows in chunks():
-        curl = curl_chunk(sc0, ex, wz, wy)
-        for c in range(3):
-            mid0[c, rows, :] = mid1[c, rows, :] + curl[c]
-    stage_v(B, mid0)
-    bv = send_v(B)
+            tot0[c, rows, :] = tot1[c, rows, :] - DT * curl[c] + PDT * lj
 
     for ex, rows in chunks():
         curl = curl_chunk(e1, ex, wz, wy)
@@ -476,14 +450,12 @@
             h2[c, rows, :] = h1[c, rows, :] - DT * curl[c]
     for ex, rows in chunks():
         curl = curl_chunk(h2, ex, wz, wy)
-        node, early = None, None
+        node = None
         for c in range(3):
             current = drude[rows, :] * (DECAY * jb[c, rows, :].astype(F32) + PDT * e1[c, rows, :])
             term = q[c, rows, :] * (curl[c] - current)
             node = term if node is None else node + term
-            term = tot0[c, rows, :] * (e1[c, rows, :] - e0[c, rows, :])
-            early = term if early is None else early + term
-        part[rows, :] = node + step[rows, :] * early
+        part[rows, :] = node
     back = LIFT * LIFT * DT
     for s in SIDES:
         x, y = X_FACE[s], Y_FACE[s]
@@ -493,7 +465,7 @@
     arrived(marks)
     mark(x_at, [idr[s, ey : ey + 1, 0:EZ] for s in SIDES for ey in range(EY)])
     mark(y_at, [idr[2 + s, ex : ex + 1, 0:EZ] for s in SIDES for ex in range(EX)])
-    mark(c_at, [idr[4 + k, 0:1, 0:EZ] for k in range(4)])
+    mark(c_at, [cr[0, k, 6:7, 0:EZ].astype(jnp.int32) for k in range(4)])
     xa = [-FACE[s] * DT * e1[2, X_FACE[s], :] for s in SIDES]
     xb = [FACE[s] * DT * e1[1, X_FACE[s], :] for s in SIDES]
     ya = [FACE[s] * DT * e1[2, Y_FACE[s], :] for s in SIDES]
@@ -517,36 +489,64 @@
 
     xaz, yaz = [along_z(v) for v in xa], [along_z(v) for v in ya]
     xby, ybx = along_rows(xb), along_rows(yb)
+    for s in SIDES:
+        xt[s] = xby[s] - xaz[s]
+        yt[s] = yaz[s] - ybx[s]
+
     in_wt.wait()
     in_wm.wait()
-    layers = []
-    for ex in range(EX):
-        n = [part[CHUNK * ex + NY * a : CHUNK * ex + NY * (a + 1), :] for a in range(4)]
-        layers.append(n[0] + n[3] + 5.0 * (n[1] + n[2]))
     scale = -1.0 / (216.0 * 8.0 * DT)
 
-    def by_element(layer, count, weights):
-        high, low = split(layer)
+    def by_element(layers, count, weights):
+        n = layers[0].shape[0]
+        high, low = split(jnp.concatenate(layers, axis=0))
         w = wt[:, 0 : count * EZ]
         wide = jnp.dot(high, w, preferred_element_type=F32) + jnp.dot(
             low, w, preferred_element_type=F32
         )
-        return jnp.sum(wide * weights, axis=0, keepdims=True) * scale
-
-    def by_block(flat, at):
-        n = flat.shape[1]
-        row = lax.broadcasted_iota(jnp.int32, (16, n), 0)
-        flat = jnp.broadcast_to(flat, (16, n))
-        top = flat.astype(BF16).astype(F32)
-        mid = (flat - top).astype(BF16).astype(F32)
-        pieces = jnp.where(
-            row == 0, top, jnp.where(row == 1, mid, jnp.where(row == 2, flat - top - mid, 0.0))
-        ).astype(BF16)
-        return jnp.dot(pieces, onehot[at : at + n, :], preferred_element_type=F32)
-
-    sums = jnp.zeros((16, 128 * n_rows), F32)
-    for i, layer in enumerate(layers):
-        sums = sums + by_block(by_element(layer, EY, wm[...]), layer_len * i)
+        return [
+            jnp.sum(wide[n * i : n * (i + 1)] * weights, axis=0, keepdims=True)
+            for i in range(len(layers))
+        ]
+
+    def by_block(flats, at):
+        out = None
+        for i, flat in enumerate(flats):
+            n = flat.shape[1]
+            row = lax.broadcasted_iota(jnp.int32, (16, n), 0)
+            flat = jnp.broadcast_to(flat, (16, n))
+            top = flat.astype(BF16).astype(F32)
+            pieces = jnp.where(row == 0, top, jnp.where(row == 1, flat - top, 0.0)).astype(BF16)
+            term = jnp.dot(
+                pieces, onehot[at + n * i : at + n * (i + 1), :], preferred_element_type=F32
+            )
+            out = term if out is None else out + term
+        return out
+
+    def layers_of(values):
+        out = []
+        for ex in range(EX):
+            n = [values[CHUNK * ex + NY * a : CHUNK * ex + NY * (a + 1), :] for a in range(4)]
+            out.append(n[0] + n[3] + 5.0 * (n[1] + n[2]))
+        return out
+
+    sums[...] = by_block(by_element(layers_of(part), EY, wm[...]), 0)
+
+    arrived(av)
+    complete_faces(vxr.at[A], vyr.at[A], cr.at[0], 2, sc1, 1.0)
+    add_faces(vxr.at[A], vyr.at[A], tot0, by_dt)
+    for c in range(3):
+        sc0[c] = step[...] * tot0[c]
+    stage_u(B, sc0)
+    stage_corners(1, 0, sc0)
+    bu = send_u(B, sc0)
+    bc = send_corners(1)
+    early = None
+    for c in range(3):
+        term = sc0[c] * (e1[c] - e0[c])
+        early = term if early is None else early + term
+    part[...] = early
+    sums[...] += by_block(by_element(layers_of(part), EY, wm[...]), 0)
 
     arrived(ws)
     planes = []
@@ -554,14 +554,16 @@
         w = wxr.at[s]
         hy, hz = h2[1, X_FACE[s], :], h2[2, X_FACE[s], :]
         planes.append(
-            w[1] * (xby[s] - xaz[s]) - w[2] * xb[s] + w[3] * xa[s]
+            w[1] * xt[s] - w[2] * (FACE[s] * DT * e1[1, X_FACE[s], :])
+            - w[3] * (FACE[s] * DT * e1[2, X_FACE[s], :])
             + FACE[s] * w[0] * (uxr[A, s, 0] * hz - uxr[A, s, 1] * hy)
         )
     for s in SIDES:
         w = wyr.at[s]
         hx, hz = h2[0, Y_FACE[s], :], h2[2, Y_FACE[s], :]
         planes.append(
-            w[1] * (yaz[s] - ybx[s]) + w[2] * yb[s] - w[3] * ya[s]
+            w[1] * yt[s] - w[2] * (FACE[s] * DT * e1[0, Y_FACE[s], :])
+            - w[3] * (FACE[s] * DT * e1[2, Y_FACE[s], :])
             + FACE[s] * w[0] * (uyr[A, s, 1] * hx - uyr[A, s, 0] * hz)
         )
     for s in SIDES:
@@ -570,20 +572,18 @@
             planes.append(
                 (-FACE[s] * FACE[t] * DT)
                 * (
-                    wcr[2 * s + t, 1:2, :] * e1[0, row : row + 1, :]
-                    + wcr[2 * s + t, 0:1, :] * e1[1, row : row + 1, :]
+                    cr[0, 2 * s + t, 5:6, :] * e1[0, row : row + 1, :]
+                    + cr[0, 2 * s + t, 4:5, :] * e1[1, row : row + 1, :]
                 )
             )
-
-    for s in SIDES:
-        sums = sums + by_block(by_element(planes[s], EY, wm[...]), x_at + layer_len * s)
-    for s in SIDES:
-        flat = by_element(planes[2 + s], EX, wm[0:NX, 0 : EX * EZ])
-        sums = sums + by_block(flat, y_at + EX * EZ * s)
-    for k in range(4):
-        flat = by_element(jnp.broadcast_to(planes[4 + k], (8, NZ)), 1, 0.125)
-        sums = sums + by_block(flat, c_at + EZ * k)
-    total = jnp.sum(sums, axis=0, keepdims=True)
+    eighths = [jnp.broadcast_to(p, (8, NZ)) for p in planes[4:8]]
+    late = (
+        sums[...]
+        + by_block(by_element(planes[0:2], EY, wm[...]), x_at)
+        + by_block(by_element(planes[2:4], EX, wm[0:NX, 0 : EX * EZ]), y_at)
+        + by_block(by_element(eighths, 1, 0.125), c_at)
+    )
+    total = jnp.sum(late, axis=0, keepdims=True) * scale
     for n in range(n_rows):
         gsend[n] = total[:, 128 * n : 128 * (n + 1)]
     width = 2 * n_gy
@@ -597,6 +597,12 @@
             )
         )
 
+    for ex, rows in chunks():
+        curl = curl_chunk(sc0, ex, wz, wy)
+        for c in range(3):
+            mid0[c, rows, :] = mid1[c, rows, :] + curl[c]
+    stage_v(B, mid0)
+    bv = send_v(B)
     for c in range(3):
         oj_out[c] = (drude[...] * (DECAY * lj1[c] - sc0[c])).astype(BF16)
 
@@ -623,7 +629,7 @@
             le0[c, rows, :] = tot0[c, rows, :] - DT * curl[c]
     arrived(bv)
     arrived(bc)
-    complete_faces(vxr.at[B], vyr.at[B], cr.at[B], sc0, 1.0)
+    complete_faces(vxr.at[B], vyr.at[B], cr.at[1], 0, sc0, 1.0)
     add_faces(vxr.at[B], vyr.at[B], le0, by_dt)
     for c in range(3):
         oe_out[c] = le0[c].astype(BF16)
@@ -664,12 +670,11 @@
     dma = pltpu.SemaphoreType.DMA
     x_faces = pltpu.VMEM((3, 2, 2, NY, NZ), F32)
     y_faces = pltpu.VMEM((3, 2, 2, NX, NZ), F32)
-    corners = pltpu.VMEM((3, 4, 2, NZ), F32)
+    corners = pltpu.VMEM((2, 4, 8, NZ), F32)
     weights = [
         pltpu.VMEM((2, 4, NY, NZ), F32),
         pltpu.VMEM((2, 4, NX, NZ), F32),
-        pltpu.VMEM((4, 2, NZ), F32),
-        pltpu.VMEM((8, 8, 128), jnp.int32),
+        pltpu.VMEM((4, 8, 128), jnp.int32),
     ]
     marked = EX * EY * EZ + 2 * EY * EZ + 2 * EX * EZ + 4 * EZ
     oe, oh, oj, grad = pl.pallas_call(
@@ -687,6 +692,9 @@
             plane32,
             plane32,
             plane32,
+            pltpu.VMEM((2, NY, NZ), F32),
+            pltpu.VMEM((2, NX, NZ), F32),
+            pltpu.VMEM((16, 128 * n_rows), F32),
             pltpu.VMEM((marked, 128 * n_rows), BF16),
             y_faces, x_faces, y_faces, corners,
             x_faces, y_faces, x_faces, y_faces, corners,
@@ -697,8 +705,8 @@
             pltpu.VMEM((1, 128), F32),
             pltpu.VMEM((n_gy, 1, 128), F32),
             dma((13,)),
-            dma((3, 4)), dma((3, 4)), dma((3, 4)), dma((3, 4)), dma((3, 4)), dma((3, 4)),
-            dma((8,)), dma((8,)), dma((8,)), dma((8,)),
+            dma((3, 4)), dma((3, 4)), dma((3, 4)), dma((3, 4)), dma((2, 4)), dma((2, 4)),
+            dma((4,)), dma((4,)), dma((4,)), dma((4,)),
             dma((n_gx,)), dma((n_gx,)), dma((n_gy,)), dma((n_gy,)),
         ],
         compiler_params=pltpu.CompilerParams(

time: 37.3 us -> 35.7 us (0.957)
  Pallas kernels: 36.5 us -> 34.9 us
    pallas_call x1, Pallas kernels: 35.1 us -> 33.6 us  [per_device(): pl.pallas_call(functools.partial(kernel, n_gx, n_gy), out_shape=(pltpu.VM...]
where the time goes in v3:
time: 35.7 us; the launch traced here: 35.6 us
  Pallas kernels  34.9 us (98%)
  between operations  0.64 us (2%)
    pallas_call x1, Pallas kernels, per_device(): pl.pallas_call(functools.partial(kernel, n_gx, n_gy), out_shape=(pltpu.VM...  33.6 us
    pallas_call x1, Pallas kernels, per_device(): pl.pallas_call(write_out, out_shape=(out16, out16, out16, jax.ShapeDtypeS...  1.37 us

profile of v3, /device:TPU:1, one launch (start us, length us, event | category | flops | bytes accessed | tf_op | source)
XLA Modules:
  0.0 35.6 jit_solution(6701640690423151800)
XLA Ops:
  0.6 33.6 %shard_map.156 = (bf16[3,288,128]{2,1,0:T(8,128)(2,1)S(1)}, bf16[3,288,128]{2,1,0:T(8,128)(2,1)S(1)}, bf16[3,288,128]{2,1,0:T(8,128)(2,1)S(1)}, f32[1,128]{1,0:T(1,128)S(1)}) custom-call(bf16[3,288,128]{2,1,0:T(8,128)(2,1)} %bitcast.10, bf16[3,288,128]{2,1,0:T(8,128)(2,1)} %bitcast.11, bf16[3,288,128]{2,1,0:T(8,128)(2,1)} %bitcast.12, ...), custom_call_target="tpu_custom_call" | custom-call | tf_op jit(solution)/shard_map/pallas_call | solution.py:680
  34.2 1.4 %shard_map.157 = (bf16[3,288,128]{2,1,0:T(8,128)(2,1)}, bf16[3,288,128]{2,1,0:T(8,128)(2,1)}, bf16[3,288,128]{2,1,0:T(8,128)(2,1)}, f32[2]{0:T(128)}) custom-call(bf16[3,288,128]{2,1,0:T(8,128)(2,1)S(1)} %get-tuple-element.12.e_in, bf16[3,288,128]{2,1,0:T(8,128)(2,1)S(1)} %get-tuple-element.13.h_in, bf16[3,288,128]{2,1,0:T(8,128)(2,1)S(1)} %get-tuple-element.14.j_in, ...), custom_call_target="tpu_custom_call" | custom-call | tf_op jit(solution)/shard_map/pallas_call | solution.py:716

commit v4 on v3

--- a/solution.py
+++ b/solution.py
@@ -139,6 +139,18 @@
 F, A, B = 0, 1, 2
 
 
+def gx_steps(n):
+    return sorted({d % n for step in (1, 4) if step < n for d in (step, -step)} - {0})
+
+
+def gx_waves(n):
+    known, waves = {0, *gx_steps(n)}, 0
+    while len(known) < n or not waves:
+        known |= {(a + b) % n for a in known for b in gx_steps(n)}
+        waves += 1
+    return waves
+
+
 def chunks():
     return [(ex, slice(CHUNK * ex, CHUNK * (ex + 1))) for ex in range(EX)]
 
@@ -181,7 +193,7 @@
     wxs, wys, ids, wxr, wyr, idr,
     gsend, grecv, msend, mrecv,
     in_sem, u_send, u_recv, v_send, v_recv, c_send, c_recv,
-    w_send, w_recv, i_send, i_recv, g_send_sem, g_recv_sem, m_send_sem, m_recv_sem,
+    w_send, w_recv, i_send, i_recv, g_send_sem, g_recv_sem, m_send_sem, m_recv_sem, heard,
 ):
     gx, gy = lax.axis_index("gx"), lax.axis_index("gy")
     near_x = (lax.rem(gx + n_gx - 1, n_gx), lax.rem(gx + 1, n_gx))
@@ -192,17 +204,17 @@
         copy.start()
         return copy
 
+    barrier = pltpu.get_barrier_semaphore()
+    near = [(lax.rem(gx + d, n_gx), gy) for d in gx_steps(n_gx)]
+    peers = near + [(gx, lax.rem(gy + k, n_gy)) for k in range(1, n_gy)]
+    peers += [(near_x[a], near_y[b]) for a in SIDES for b in SIDES]
+    for peer in peers:
+        pl.semaphore_signal(barrier, inc=1, device_id=peer, device_id_type=MESH)
+
     in_e = load(0, e_in, eb)
     in_h = load(7, h_in, hb)
     in_wz = load(5, wz_in, wz)
     in_wy = load(6, wy_in, wy)
-
-    barrier = pltpu.get_barrier_semaphore()
-    peers = [(near_x[a], near_y[b]) for a in SIDES for b in SIDES]
-    peers += [(lax.rem(gx + k, n_gx), gy) for k in range(1, n_gx)]
-    peers += [(gx, lax.rem(gy + k, n_gy)) for k in range(1, n_gy)]
-    for peer in peers:
-        pl.semaphore_signal(barrier, inc=1, device_id=peer, device_id_type=MESH)
 
     in_le = load(1, le_in, leb)
     in_lj = load(2, lj_in, ljb)
@@ -355,7 +367,14 @@
     pl.semaphore_wait(barrier, len(peers))
     fu = send_u(F, e0)
     fv = send_v(F)
+
+    def pass_on(wave):
+        for peer in near:
+            pl.semaphore_signal(heard.at[wave], inc=1, device_id=peer, device_id_type=MESH)
+
     rc = send_corners(0)
+    waves = gx_waves(n_gx)
+    pass_on(0)
     au = send_u(A, sc1)
     av = send_v(A)
     marks = []
@@ -421,6 +440,10 @@
     y_at = x_at + 2 * layer_len
     c_at = y_at + 2 * EX * EZ
 
+    pl.semaphore_wait(heard.at[0], len(near))
+    if waves > 1:
+        pass_on(1)
+
     in_j.wait()
     arrived(fu)
     add_faces(uxr.at[F], uyr.at[F], h1, by_dt)
@@ -586,6 +609,10 @@
     total = jnp.sum(late, axis=0, keepdims=True) * scale
     for n in range(n_rows):
         gsend[n] = total[:, 128 * n : 128 * (n + 1)]
+    for wave in range(1, waves):
+        pl.semaphore_wait(heard.at[wave], len(near))
+        if wave + 1 < waves:
+            pass_on(wave + 1)
     width = 2 * n_gy
     per_row = 128 // width
     phase1 = []
@@ -708,6 +735,7 @@
             dma((3, 4)), dma((3, 4)), dma((3, 4)), dma((3, 4)), dma((2, 4)), dma((2, 4)),
             dma((4,)), dma((4,)), dma((4,)), dma((4,)),
             dma((n_gx,)), dma((n_gx,)), dma((n_gy,)), dma((n_gy,)),
+            pltpu.SemaphoreType.REGULAR((gx_waves(n_gx),)),
         ],
         compiler_params=pltpu.CompilerParams(
             collective_id=0, has_side_effects=True, vmem_limit_bytes=60 * 1024 * 1024

time: 35.7 us -> 34.9 us (0.978)
  Pallas kernels: 34.9 us -> 34.1 us
    pallas_call x1, Pallas kernels: 33.6 us -> 32.7 us  [per_device(): pl.pallas_call(functools.partial(kernel, n_gx, n_gy), out_shape=(pltpu.VM...]
where the time goes in v4:
time: 34.9 us; the launch traced here: 34.7 us
  Pallas kernels  34.1 us (98%)
  between operations  0.64 us (2%)
    pallas_call x1, Pallas kernels, per_device(): pl.pallas_call(functools.partial(kernel, n_gx, n_gy), out_shape=(pltpu.VM...  32.7 us
    pallas_call x1, Pallas kernels, per_device(): pl.pallas_call(write_out, out_shape=(out16, out16, out16, jax.ShapeDtypeS...  1.37 us

profile of v4, /device:TPU:1, one launch (start us, length us, event | category | flops | bytes accessed | tf_op | source)
XLA Modules:
  0.0 34.7 jit_solution(12021227957982485917)
XLA Ops:
  0.6 32.7 %shard_map.156 = (bf16[3,288,128]{2,1,0:T(8,128)(2,1)S(1)}, bf16[3,288,128]{2,1,0:T(8,128)(2,1)S(1)}, bf16[3,288,128]{2,1,0:T(8,128)(2,1)S(1)}, f32[1,128]{1,0:T(1,128)S(1)}) custom-call(bf16[3,288,128]{2,1,0:T(8,128)(2,1)} %bitcast.10, bf16[3,288,128]{2,1,0:T(8,128)(2,1)} %bitcast.11, bf16[3,288,128]{2,1,0:T(8,128)(2,1)} %bitcast.12, ...), custom_call_target="tpu_custom_call" | custom-call | tf_op jit(solution)/shard_map/pallas_call | solution.py:707
  33.4 1.4 %shard_map.157 = (bf16[3,288,128]{2,1,0:T(8,128)(2,1)}, bf16[3,288,128]{2,1,0:T(8,128)(2,1)}, bf16[3,288,128]{2,1,0:T(8,128)(2,1)}, f32[2]{0:T(128)}) custom-call(bf16[3,288,128]{2,1,0:T(8,128)(2,1)S(1)} %get-tuple-element.12.e_in, bf16[3,288,128]{2,1,0:T(8,128)(2,1)S(1)} %get-tuple-element.13.h_in, bf16[3,288,128]{2,1,0:T(8,128)(2,1)S(1)} %get-tuple-element.14.j_in, ...), custom_call_target="tpu_custom_call" | custom-call | tf_op jit(solution)/shard_map/pallas_call | solution.py:744

commit v5 on v4

--- a/solution.py
+++ b/solution.py
@@ -323,6 +323,15 @@
     cs[...] = jnp.zeros_like(cs)
     stage_corners(0, 0, e0)
 
+    pl.semaphore_wait(barrier, len(peers))
+    fu = send_u(F, e0)
+    fv = send_v(F)
+
+    def pass_on(wave):
+        for peer in near:
+            pl.semaphore_signal(heard.at[wave], inc=1, device_id=peer, device_id_type=MESH)
+
+
     in_mat.wait()
     in_eps.wait()
     zpick = (
@@ -364,14 +373,6 @@
         for t in SIDES:
             line = blk[(EX - 1) * s, (EY - 1) * t : (EY - 1) * t + 1, :]
             cs[0, 2 * s + t, 6:7, 0:EZ] = line.astype(F32)
-    pl.semaphore_wait(barrier, len(peers))
-    fu = send_u(F, e0)
-    fv = send_v(F)
-
-    def pass_on(wave):
-        for peer in near:
-            pl.semaphore_signal(heard.at[wave], inc=1, device_id=peer, device_id_type=MESH)
-
     rc = send_corners(0)
     waves = gx_waves(n_gx)
     pass_on(0)

time: 34.9 us -> 34.5 us (0.989)
  no operation moved by 1% of the time
where the time goes in v5:
time: 34.5 us; the launch traced here: 34.4 us
  Pallas kernels  33.8 us (98%)
  between operations  0.64 us (2%)
    pallas_call x1, Pallas kernels, per_device(): pl.pallas_call(functools.partial(kernel, n_gx, n_gy), out_shape=(pltpu.VM...  32.4 us
    pallas_call x1, Pallas kernels, per_device(): pl.pallas_call(write_out, out_shape=(out16, out16, out16, jax.ShapeDtypeS...  1.37 us

profile of v5, /device:TPU:1, one launch (start us, length us, event | category | flops | bytes accessed | tf_op | source)
XLA Modules:
  0.0 34.4 jit_solution(1197922668565032294)
XLA Ops:
  0.6 32.4 %shard_map.156 = (bf16[3,288,128]{2,1,0:T(8,128)(2,1)S(1)}, bf16[3,288,128]{2,1,0:T(8,128)(2,1)S(1)}, bf16[3,288,128]{2,1,0:T(8,128)(2,1)S(1)}, f32[1,128]{1,0:T(1,128)S(1)}) custom-call(bf16[3,288,128]{2,1,0:T(8,128)(2,1)} %bitcast.10, bf16[3,288,128]{2,1,0:T(8,128)(2,1)} %bitcast.11, bf16[3,288,128]{2,1,0:T(8,128)(2,1)} %bitcast.12, ...), custom_call_target="tpu_custom_call" | custom-call | tf_op jit(solution)/shard_map/pallas_call | solution.py:708
  33.1 1.4 %shard_map.157 = (bf16[3,288,128]{2,1,0:T(8,128)(2,1)}, bf16[3,288,128]{2,1,0:T(8,128)(2,1)}, bf16[3,288,128]{2,1,0:T(8,128)(2,1)}, f32[2]{0:T(128)}) custom-call(bf16[3,288,128]{2,1,0:T(8,128)(2,1)S(1)} %get-tuple-element.12.e_in, bf16[3,288,128]{2,1,0:T(8,128)(2,1)S(1)} %get-tuple-element.13.h_in, bf16[3,288,128]{2,1,0:T(8,128)(2,1)S(1)} %get-tuple-element.14.j_in, ...), custom_call_target="tpu_custom_call" | custom-call | tf_op jit(solution)/shard_map/pallas_call | solution.py:745

commit v6 on v5

--- a/solution.py
+++ b/solution.py
@@ -554,7 +554,21 @@
             out.append(n[0] + n[3] + 5.0 * (n[1] + n[2]))
         return out
 
-    sums[...] = by_block(by_element(layers_of(part), EY, wm[...]), 0)
+    eighths = []
+    for s in SIDES:
+        for t in SIDES:
+            row = CORNER[s][t]
+            line = (
+                (-FACE[s] * FACE[t] * DT)
+                * (
+                    cr[0, 2 * s + t, 5:6, :] * e1[0, row : row + 1, :]
+                    + cr[0, 2 * s + t, 4:5, :] * e1[1, row : row + 1, :]
+                )
+            )
+            eighths.append(jnp.broadcast_to(line, (8, NZ)))
+    sums[...] = by_block(by_element(layers_of(part), EY, wm[...]), 0) + by_block(
+        by_element(eighths, 1, 0.125), c_at
+    )
 
     arrived(av)
     complete_faces(vxr.at[A], vyr.at[A], cr.at[0], 2, sc1, 1.0)
@@ -590,22 +604,10 @@
             - w[3] * (FACE[s] * DT * e1[2, Y_FACE[s], :])
             + FACE[s] * w[0] * (uyr[A, s, 1] * hx - uyr[A, s, 0] * hz)
         )
-    for s in SIDES:
-        for t in SIDES:
-            row = CORNER[s][t]
-            planes.append(
-                (-FACE[s] * FACE[t] * DT)
-                * (
-                    cr[0, 2 * s + t, 5:6, :] * e1[0, row : row + 1, :]
-                    + cr[0, 2 * s + t, 4:5, :] * e1[1, row : row + 1, :]
-                )
-            )
-    eighths = [jnp.broadcast_to(p, (8, NZ)) for p in planes[4:8]]
     late = (
         sums[...]
         + by_block(by_element(planes[0:2], EY, wm[...]), x_at)
         + by_block(by_element(planes[2:4], EX, wm[0:NX, 0 : EX * EZ]), y_at)
-        + by_block(by_element(eighths, 1, 0.125), c_at)
     )
     total = jnp.sum(late, axis=0, keepdims=True) * scale
     for n in range(n_rows):

time: 34.5 us -> 34.6 us (level)
  no operation moved by 1% of the time
where the time goes in v6:
time: 34.6 us; the launch traced here: 34.5 us
  Pallas kernels  33.9 us (98%)
  between operations  0.64 us (2%)
    pallas_call x1, Pallas kernels, per_device(): pl.pallas_call(functools.partial(kernel, n_gx, n_gy), out_shape=(pltpu.VM...  32.5 us
    pallas_call x1, Pallas kernels, per_device(): pl.pallas_call(write_out, out_shape=(out16, out16, out16, jax.ShapeDtypeS...  1.37 us

profile of v6, /device:TPU:1, one launch (start us, length us, event | category | flops | bytes accessed | tf_op | source)
XLA Modules:
  0.0 34.5 jit_solution(7841948976970733365)
XLA Ops:
  0.6 32.5 %shard_map.156 = (bf16[3,288,128]{2,1,0:T(8,128)(2,1)S(1)}, bf16[3,288,128]{2,1,0:T(8,128)(2,1)S(1)}, bf16[3,288,128]{2,1,0:T(8,128)(2,1)S(1)}, f32[1,128]{1,0:T(1,128)S(1)}) custom-call(bf16[3,288,128]{2,1,0:T(8,128)(2,1)} %bitcast.10, bf16[3,288,128]{2,1,0:T(8,128)(2,1)} %bitcast.11, bf16[3,288,128]{2,1,0:T(8,128)(2,1)} %bitcast.12, ...), custom_call_target="tpu_custom_call" | custom-call | tf_op jit(solution)/shard_map/pallas_call | solution.py:710
  33.1 1.4 %shard_map.157 = (bf16[3,288,128]{2,1,0:T(8,128)(2,1)}, bf16[3,288,128]{2,1,0:T(8,128)(2,1)}, bf16[3,288,128]{2,1,0:T(8,128)(2,1)}, f32[2]{0:T(128)}) custom-call(bf16[3,288,128]{2,1,0:T(8,128)(2,1)S(1)} %get-tuple-element.12.e_in, bf16[3,288,128]{2,1,0:T(8,128)(2,1)S(1)} %get-tuple-element.13.h_in, bf16[3,288,128]{2,1,0:T(8,128)(2,1)S(1)} %get-tuple-element.14.j_in, ...), custom_call_target="tpu_custom_call" | custom-call | tf_op jit(solution)/shard_map/pallas_call | solution.py:747

commit v7 on v6

--- a/solution.py
+++ b/solution.py
@@ -570,6 +570,18 @@
         by_element(eighths, 1, 0.125), c_at
     )
 
+    arrived([c for i, c in enumerate(ws) if i % 2])
+    planes = []
+    for s in SIDES:
+        w = wyr.at[s]
+        hx, hz = h2[0, Y_FACE[s], :], h2[2, Y_FACE[s], :]
+        planes.append(
+            w[1] * yt[s] - w[2] * (FACE[s] * DT * e1[0, Y_FACE[s], :])
+            - w[3] * (FACE[s] * DT * e1[2, Y_FACE[s], :])
+            + FACE[s] * w[0] * (uyr[A, s, 1] * hx - uyr[A, s, 0] * hz)
+        )
+    sums[...] += by_block(by_element(planes, EX, wm[0:NX, 0 : EX * EZ]), y_at)
+
     arrived(av)
     complete_faces(vxr.at[A], vyr.at[A], cr.at[0], 2, sc1, 1.0)
     add_faces(vxr.at[A], vyr.at[A], tot0, by_dt)
@@ -586,7 +598,7 @@
     part[...] = early
     sums[...] += by_block(by_element(layers_of(part), EY, wm[...]), 0)
 
-    arrived(ws)
+    arrived([c for i, c in enumerate(ws) if i % 2 == 0])
     planes = []
     for s in SIDES:
         w = wxr.at[s]
@@ -596,18 +608,9 @@
             - w[3] * (FACE[s] * DT * e1[2, X_FACE[s], :])
             + FACE[s] * w[0] * (uxr[A, s, 0] * hz - uxr[A, s, 1] * hy)
         )
-    for s in SIDES:
-        w = wyr.at[s]
-        hx, hz = h2[0, Y_FACE[s], :], h2[2, Y_FACE[s], :]
-        planes.append(
-            w[1] * yt[s] - w[2] * (FACE[s] * DT * e1[0, Y_FACE[s], :])
-            - w[3] * (FACE[s] * DT * e1[2, Y_FACE[s], :])
-            + FACE[s] * w[0] * (uyr[A, s, 1] * hx - uyr[A, s, 0] * hz)
-        )
     late = (
         sums[...]
-        + by_block(by_element(planes[0:2], EY, wm[...]), x_at)
-        + by_block(by_element(planes[2:4], EX, wm[0:NX, 0 : EX * EZ]), y_at)
+        + by_block(by_element(planes, EY, wm[...]), x_at)
     )
     total = jnp.sum(late, axis=0, keepdims=True) * scale
     for n in range(n_rows):

time: 34.6 us -> 34.9 us (level)
  no operation moved by 1% of the time
where the time goes in v7:
time: 34.9 us; the launch traced here: 34.8 us
  Pallas kernels  34.1 us (98%)
  between operations  0.64 us (2%)
    pallas_call x1, Pallas kernels, per_device(): pl.pallas_call(functools.partial(kernel, n_gx, n_gy), out_shape=(pltpu.VM...  32.8 us
    pallas_call x1, Pallas kernels, per_device(): pl.pallas_call(write_out, out_shape=(out16, out16, out16, jax.ShapeDtypeS...  1.37 us

profile of v7, /device:TPU:1, one launch (start us, length us, event | category | flops | bytes accessed | tf_op | source)
XLA Modules:
  0.0 34.8 jit_solution(12450182250249194777)
XLA Ops:
  0.6 32.8 %shard_map.156 = (bf16[3,288,128]{2,1,0:T(8,128)(2,1)S(1)}, bf16[3,288,128]{2,1,0:T(8,128)(2,1)S(1)}, bf16[3,288,128]{2,1,0:T(8,128)(2,1)S(1)}, f32[1,128]{1,0:T(1,128)S(1)}) custom-call(bf16[3,288,128]{2,1,0:T(8,128)(2,1)} %bitcast.10, bf16[3,288,128]{2,1,0:T(8,128)(2,1)} %bitcast.11, bf16[3,288,128]{2,1,0:T(8,128)(2,1)} %bitcast.12, ...), custom_call_target="tpu_custom_call" | custom-call | tf_op jit(solution)/shard_map/pallas_call | solution.py:713
  33.4 1.4 %shard_map.157 = (bf16[3,288,128]{2,1,0:T(8,128)(2,1)}, bf16[3,288,128]{2,1,0:T(8,128)(2,1)}, bf16[3,288,128]{2,1,0:T(8,128)(2,1)}, f32[2]{0:T(128)}) custom-call(bf16[3,288,128]{2,1,0:T(8,128)(2,1)S(1)} %get-tuple-element.12.e_in, bf16[3,288,128]{2,1,0:T(8,128)(2,1)S(1)} %get-tuple-element.13.h_in, bf16[3,288,128]{2,1,0:T(8,128)(2,1)S(1)} %get-tuple-element.14.j_in, ...), custom_call_target="tpu_custom_call" | custom-call | tf_op jit(solution)/shard_map/pallas_call | solution.py:750
